TPU v7x, 128 devices: a whole 4x4x4 slice. The times are simulated.
128 devices in a mesh: gx: 16 (over z_hi, x, core), gy: 8 (over z_lo, y).
Axes of the slice: x: 4, y: 4, z: 4 (z_hi: 2, z_lo: 2; z = z_hi * 2 + z_lo), core: 2. Of those that a mesh axis runs over, the one named last changes fastest.
Arguments:
- fields: bfloat16 [8, 64, 32, 64, 128], P(None, None, 'gx', 'gy'), may hold values from -6 to 6
- depth_kernel: bfloat16 [64, 3, 3, 3], replicated, may hold values from -1.25 to 1.25
- point_in: bfloat16 [256, 64], replicated, may hold values from -0.75 to 0.75
- point_out: bfloat16 [64, 256], replicated, may hold values from -0.375 to 0.375
- down_kernel: bfloat16 [128, 64, 2, 2, 2], replicated, may hold values from -0.25 to 0.25
- cotangent: bfloat16 [16, 8, 1, 128, 4, 8, 64], P('gx', 'gy'), may hold values from -6 to 6
Outputs:
- coarse: bfloat16 [16, 8, 1, 128, 4, 8, 64], P('gx', 'gy')
- grad_fields: bfloat16 [8, 64, 32, 64, 128], P(None, None, 'gx', 'gy')
- grad_depth_kernel: float32 [64, 3, 3, 3], replicated
- grad_point_in: float32 [256, 64], replicated
- grad_point_out: float32 [64, 256], replicated
- grad_down_kernel: float32 [128, 64, 2, 2, 2], replicated
All inputs are finite; a program needn't handle non-finite values.
Results may differ from a plain program's by a relative error of at most 0.0066.
Values may be sent and summed in bfloat16 or wider, within the bound.
A program may use at most 192 MiB of HBM per device.

v0:
```python
import math

import jax
import jax.numpy as jnp
from jax import lax
from jax.sharding import PartitionSpec as P

GRIDC = 4


def padded_2(x, sides, width):
    for axis, dim in sides:
        peers, length = (lax.axis_size(axis), x.shape[dim])
        up = [(i, (i + 1) % peers) for i in range(peers - 1)]
        down = [(j, i) for i, j in up]
        last = lax.slice_in_dim(x, length - width, length, axis=dim)
        initial = lax.slice_in_dim(x, 0, width, axis=dim)
        before = lax.ppermute(last, axis, up)
        after = lax.ppermute(initial, axis, down)
        x = jnp.concatenate([before, x, after], axis=dim)
    return x


def shifted(block, axis, distance):
    devices = range(lax.axis_size(axis))
    route = [((i - distance) % len(devices), i) for i in devices]
    return lax.ppermute(block, axis, route)


def gelu_slope(values):
    outputs, pullback = jax.vjp(jax.nn.gelu, values)
    return pullback(jnp.ones_like(outputs))[0]


def depth_conv(padded, weights, span_x, span_y, span_z):
    summed = jnp.zeros(padded.shape[:-3] + (span_x, span_y, span_z), jnp.float32)
    for offset_x in range(3):
        for offset_y in range(3):
            for offset_z in range(3):
                factor = weights[:, offset_x, offset_y, offset_z].astype(jnp.float32)[
                    :, None, None, None
                ]
                window = padded[
                    ...,
                    offset_x : offset_x + span_x,
                    offset_y : offset_y + span_y,
                    offset_z : offset_z + span_z,
                ]
                summed = summed + factor * window
    return summed


def pad_rims(blocks):
    widened = padded_2(blocks, (("gx", 2), ("gy", 3)), 1)
    return jnp.pad(widened, ((0, 0), (0, 0), (0, 0), (0, 0), (1, 1)))


def move_x(part, amount):
    return shifted(part, "gx", amount)


def move_y(part, amount):
    return shifted(part, "gy", amount)


def regroup(blocks, position, along_x):
    group_size = blocks.shape[0]
    mover = move_x if along_x else move_y
    member = position % group_size
    received = [lax.dynamic_index_in_dim(blocks, member, 0, keepdims=False)]
    for offset in range(1, group_size):
        outgoing = lax.dynamic_index_in_dim(
            blocks, (member + offset) % group_size, 0, keepdims=False
        )
        near_part = mover(outgoing, offset)
        far_part = mover(outgoing, offset - group_size)
        received.append(jnp.where(member >= offset, near_part, far_part))
    stacked = jnp.stack(received)
    reorder = (member - jnp.arange(group_size, dtype=jnp.int32)) % group_size
    return jnp.take(stacked, reorder, axis=0)


def per_device(fields, depth_kernel, point_in, point_out, down_kernel, cotangent):
    samples, chans, span_x, span_y, span_z = fields.shape
    half_x, half_y, half_z = (span_x // 2, span_y // 2, span_z // 2)
    out_chans = down_kernel.shape[0]
    group_x = lax.axis_size("gx") // GRIDC
    group_y = lax.axis_size("gy") // GRIDC
    index_x = lax.axis_index("gx")
    index_y = lax.axis_index("gy")
    padded = pad_rims(fields)
    depth_out = depth_conv(padded, depth_kernel, span_x, span_y, span_z).astype(jnp.bfloat16)
    flat_depth = depth_out.reshape(samples, chans, -1)
    flat_fields = fields.reshape(samples, chans, -1)

    def forward_one(inputs):
        depth_one, field_one = inputs
        preact = jnp.dot(point_in, depth_one, preferred_element_type=jnp.float32)
        active = jax.nn.gelu(preact).astype(jnp.bfloat16)
        branch = jnp.dot(point_out, active, preferred_element_type=jnp.float32)
        return (field_one.astype(jnp.float32) + branch).astype(jnp.bfloat16)

    merged = lax.map(forward_one, (flat_depth, flat_fields))
    patches = (
        merged.reshape(samples, chans, half_x, 2, half_y, 2, half_z, 2)
        .transpose(0, 1, 3, 5, 7, 2, 4, 6)
        .reshape(samples, chans * 8, -1)
    )
    down_mat = down_kernel.reshape(out_chans, chans * 8)
    reduced = jnp.einsum(
        "ok,skn->son", down_mat, patches, preferred_element_type=jnp.float32
    ).astype(jnp.bfloat16)
    reduced = reduced.reshape(samples, out_chans, half_x, half_y, half_z)
    sectioned = regroup(
        reduced.reshape(group_x, samples // group_x, out_chans, half_x, half_y, half_z),
        index_x,
        True,
    )
    wide_x = group_x * half_x
    sectioned = sectioned.transpose(1, 2, 0, 3, 4, 5).reshape(
        samples // group_x, out_chans, wide_x, half_y, half_z
    )
    per_group = samples // (group_x * group_y)
    sectioned = regroup(
        sectioned.reshape(group_y, per_group, out_chans, wide_x, half_y, half_z), index_y, False
    )
    coarse = sectioned.transpose(1, 2, 3, 0, 4, 5).reshape(
        per_group, out_chans, wide_x, group_y * half_y, half_z
    )[None, None]
    incoming = (
        cotangent[0, 0]
        .reshape(per_group, out_chans, wide_x, group_y, half_y, half_z)
        .transpose(3, 0, 1, 2, 4, 5)
    )
    incoming = regroup(incoming, index_y, False).reshape(
        group_y * per_group, out_chans, wide_x, half_y, half_z
    )
    incoming = incoming.reshape(
        group_y * per_group, out_chans, group_x, half_x, half_y, half_z
    ).transpose(2, 0, 1, 3, 4, 5)
    grad_down = regroup(incoming, index_x, True).reshape(samples, out_chans, -1)
    grad_patch = jnp.einsum("ok,son->skn", down_mat, grad_down, preferred_element_type=jnp.float32)
    grad_merged = (
        grad_patch.reshape(samples, chans, 2, 2, 2, half_x, half_y, half_z)
        .transpose(0, 1, 5, 2, 6, 3, 7, 4)
        .reshape(samples, chans, -1)
        .astype(jnp.bfloat16)
    )
    grad_downw = jnp.einsum("son,skn->ok", grad_down, patches, preferred_element_type=jnp.float32)

    def backward_one(inputs):
        depth_one, merged_grad = inputs
        preact = jnp.dot(point_in, depth_one, preferred_element_type=jnp.float32)
        active = jax.nn.gelu(preact).astype(jnp.bfloat16)
        grad_active = jnp.dot(point_out.T, merged_grad, preferred_element_type=jnp.float32)
        grad_pre = (grad_active * gelu_slope(preact)).astype(jnp.bfloat16)
        outw = jnp.dot(merged_grad, active.T, preferred_element_type=jnp.float32)
        inw = jnp.dot(grad_pre, depth_one.T, preferred_element_type=jnp.float32)
        depth_grad = jnp.dot(point_in.T, grad_pre, preferred_element_type=jnp.float32).astype(
            jnp.bfloat16
        )
        return (depth_grad, outw, inw)

    grad_depth, outw_parts, inw_parts = lax.map(backward_one, (flat_depth, grad_merged))
    grad_outw = jnp.sum(outw_parts, axis=0)
    grad_inw = jnp.sum(inw_parts, axis=0)
    grad_depth = grad_depth.reshape(fields.shape)
    grad_pad = pad_rims(grad_depth)
    adjoint = depth_conv(grad_pad, depth_kernel[:, ::-1, ::-1, ::-1], span_x, span_y, span_z)
    grad_fields = (grad_merged.reshape(fields.shape).astype(jnp.float32) + adjoint).astype(
        jnp.bfloat16
    )
    columns = []
    for offset_x in range(3):
        for offset_y in range(3):
            for offset_z in range(3):
                window = padded[
                    :,
                    :,
                    offset_x : offset_x + span_x,
                    offset_y : offset_y + span_y,
                    offset_z : offset_z + span_z,
                ]
                columns.append(
                    lax.dot_general(
                        grad_depth,
                        window,
                        (((0, 2, 3, 4), (0, 2, 3, 4)), ((1,), (1,))),
                        preferred_element_type=jnp.float32,
                    )
                )
    grad_depthw = jnp.stack(columns, axis=1).reshape(chans, 3, 3, 3)
    totals = lax.psum(
        (grad_depthw, grad_inw, grad_outw, grad_downw.reshape(out_chans, chans, 2, 2, 2)),
        ("gx", "gy"),
    )
    norm_scale = 1.0 / math.sqrt(
        samples * span_x * span_y * span_z * lax.axis_size("gx") * lax.axis_size("gy")
    )
    return (
        coarse,
        grad_fields,
        totals[0] * norm_scale,
        totals[1] * norm_scale,
        totals[2] * norm_scale,
        totals[3] * norm_scale,
    )


def solution(mesh):
    placed = (
        P(None, None, "gx", "gy", None),
        P(),
        P(),
        P(),
        P(),
        P("gx", "gy", None, None, None, None, None),
    )
    return jax.shard_map(
        per_device,
        mesh=mesh,
        in_specs=placed,
        out_specs=(
            P("gx", "gy", None, None, None, None, None),
            P(None, None, "gx", "gy", None),
            P(),
            P(),
            P(),
            P(),
        ),
        check_vma=False,
    )
```

profile of v0, /device:TPU:1, one launch (start us, length us, event | category | flops | bytes accessed | tf_op | source)
XLA Modules:
  0.0 662.3 jit_solution(10778714051113016696)
XLA Ops:
  61.5 6.5 collective-permute-start.15
  68.9 10.8 %collective-permute-start.14 = (bf16[2,128,1,4,64]{1,4,3,0,2:T(8,128)(2,1)}, bf16[2,128,1,4,64]{1,4,3,0,2:T(8,128)(2,1)}, u32[]{:S(2)}, u32[]{:S(2)}) collective-permute-start(bf16[2,128,1,4,64]{1,4,3,0,2:T(8,128)(2,1)} %get-tuple-element.290), channel_id=1, source_target_pairs={{120,0},{0,8},{8,16},{16,24},{24,32},{32,40},{40,48},{48,56},{56,6... | collective-permute-start | bytes 393224 | tf_op jit(solution)/shard_map/ppermute | solution.py:27
  84.5 11.9 %select_maximum_fusion.4 = bf16[8,64,4,10,130]{1,0,4,3,2:T(8,128)(2,1)} fusion(bf16[8,64,4,1,128]{1,0,4,3,2:T(8,128)(2,1)S(1)} %copy.104, bf16[8,64,4,1,128]{1,0,4,3,2:T(8,128)(2,1)} %copy.103, bf16[8,64,1,8,128]{1,0,4,3,2:T(8,128)(2,1)S(1)} %copy.100, bf16[8,64,2,8,128]{1,0,4,3,2:T(8,128)(2,1)} %copy.99, bf16[8,64,1,8,128]{1,0,4,3,2:T(8,128)(2,1)} %copy.98), kind=kLoop, calls=%fused_computation.99 | loop fusion | flops 47923200 | bytes 10567680 | tf_op jit(solution)/shard_map/concatenate | solution.py:20
  96.6 8.8 %maximum_maximum_fusion = (bf16[8,64,4,9,128]{1,0,4,3,2:T(8,128)(2,1)}, bf16[8,64,4,9,128]{1,0,4,3,2:T(8,128)(2,1)}) fusion(bf16[8,64,1,8,128]{1,0,4,3,2:T(8,128)(2,1)S(1)} %copy.100, bf16[8,64,2,8,128]{1,0,4,3,2:T(8,128)(2,1)S(1)} %copy-done.4, bf16[8,64,1,8,128]{1,0,4,3,2:T(8,128)(2,1)S(1)} %copy-done.6, bf16[8,64,4,1,128]{1,0,4,3,2:T(8,128)(2,1)S(1)} %copy-done.11, ...), kind=kLoop, calls=%fused_computation.106 | loop fusion | flops 14155776 | bytes 14680064 | tf_op jit(solution)/shard_map/concatenate | solution.py:20
  105.7 37.4 %add_convert_fusion.1 = bf16[8,64,2,8,128]{1,0,4,3,2:T(8,128)(2,1)} fusion(bf16[8,64,2,8,128]{1,0,4,3,2:T(8,128)(2,1)} %copy.99, f32[64]{0:T(128)S(1)} %copy-done.29, f32[64]{0:T(128)S(1)} %copy-done.31, f32[64]{0:T(128)S(1)} %copy-done.35, f32[64]{0:T(128)S(1)} %copy-done.37, f32[64]{0:T(128)S(1)} %copy-done.39, f32[64]{0:T(128)S(1)} %copy-done.41, ...), kind=kLoop, calls=%fused_computation.137 | loop fusion | flops 87031808 | bytes 56630016 | tf_op jit(solution)/shard_map/convert_element_type | solution.py:92
  149.2 22.6 %while.26 = (s32[]{:T(128)}, bf16[8,64,2048]{2,1,0:T(8,128)(2,1)}, bf16[8,64,2048]{2,1,0:T(8,128)(2,1)}, bf16[8,64,2048]{2,1,0:T(8,128)(2,1)S(1)}, bf16[256,64]{...) while((s32[]{:T(128)}, bf16[8,64,2048]{2,1,0:T(8,128)(2,1)}, bf16[8,64,2048]{2,1,0:T(8,128)(2,1)}, ...), condition=%wide.region_1.2_spmd, body=%wide.region_0.1_spmd.sunk | while | flops 139329536 | bytes 853077 | solution.py:103
  171.8 6.0 copy.113
  177.8 8.2 %copy.114 = bf16[8,64,2,2,2,1,4,64]{7,6,4,3,2,1,0,5:T(4,128)(2,1)} copy(bf16[8,64,2,2,2,1,4,64]{1,0,4,7,3,6,2,5:T(8,128)(2,1)} %bitcast.478) | data formatting | bytes 4194304 | tf_op jit(solution)/shard_map/transpose | solution.py:106
  186.0 6.0 reshape.318
  197.0 5.8 collective-permute-start.7
  226.1 8.0 %copy.315 = bf16[8,64,2,2,2,1,4,64]{1,0,4,7,3,6,2,5:T(8,128)(2,1)} copy(bf16[8,64,2,2,2,1,4,64]{7,6,4,3,2,1,0,5:T(4,128)(2,1)} %convert_element_type.648) | data formatting | bytes 4194304 | tf_op jit(solution)/shard_map/convert_element_type | solution.py:170
  239.8 63.6 %while.27 = (s32[]{:T(128)}, bf16[8,64,2048]{2,1,0:T(8,128)(2,1)S(1)}, f32[8,64,256]{2,1,0:T(8,128)}, f32[8,256,64]{1,2,0:T(8,128)S(1)}, bf16[8,64,2048]{2,1,0:T...) while((s32[]{:T(128)}, ...), condition=%wide.region_3.6_spmd, body=%wide.region_2.5_spmd.sunk | while | flops 350355456 | bytes 10979441 | solution.py:164
  304.7 5.8 copy.128
  310.5 16.1 %fusion.84 = (f32[64]{0:T(128)S(1)}, f32[64]{0:T(128)S(1)}, f32[64]{0:T(128)S(1)}, f32[64]{0:T(128)S(1)}, f32[64]{0:T(128)S(1)}, /*index=5*/f32[64]{0:T(128)S(1)}, f32[64]{0:T(128)S(1)}, f32[64]{0:T(128)S(1)}) fusion(bf16[64,8,2,8,128]{0,1,4,3,2:T(8,128)(2,1)} %bitcast.468, bf16[8,64,4,9,128]{1,0,4,3,2:T(8,128)(2,1)} %get-tuple-element.280, ...), kind=kLoop, calls=%fused_computation.134 | loop fusion | flops 28311040 | bytes 18876416 | tf_op jit(solution)/shard_map/dot_general | solution.py:185
  326.6 20.8 %fusion.85 = (f32[64]{0:T(128)S(1)}, f32[64]{0:T(128)S(1)}, f32[64]{0:T(128)S(1)}, f32[64]{0:T(128)S(1)}, f32[64]{0:T(128)S(1)}, /*index=5*/f32[64]{0:T(128)S(1)...) fusion(bf16[64,8,2,8,128]{0,1,4,3,2:T(8,128)(2,1)S(1)} %bitcast, ...), kind=kLoop, calls=%fused_computation.135 | loop fusion | flops 57670528 | bytes 39850496 | tf_op jit(solution)/shard_map/dot_general | solution.py:185
  364.9 7.7 %collective-permute-start.21 = (bf16[8,64,1,8,128]{4,3,2,1,0:T(8,128)(2,1)}, bf16[8,64,1,8,128]{4,3,2,1,0:T(8,128)(2,1)}, u32[]{:S(2)}, u32[]{:S(2)}) collective-permute-start(bf16[8,64,1,8,128]{4,3,2,1,0:T(8,128)(2,1)} %copy.130), channel_id=1, source_target_pairs={{8,0},{16,8},{24,16},{32,24},{40,32},{48,40},{56,48},{64,56},{72,6... | collective-permute-start | bytes 3145736 | tf_op jit(solution)/shard_map/ppermute | solution.py:19
  374.6 6.1 copy.232
  390.5 10.4 %copy.124 = f32[8,64,1,2,4,2,64,2]{1,0,7,6,5,4,3,2:T(8,128)} copy(f32[8,64,1,2,4,2,64,2]{6,1,7,5,4,3,2,0:T(8,128)} %bitcast_convert_fusion) | data formatting | bytes 8388608 | tf_op jit(solution)/shard_map/convert_element_type | solution.py:170
  401.0 73.0 %psum.28 = f32[64,3,3,3]{0,3,2,1:T(4,128)S(1)} all-reduce(f32[64,3,3,3]{0,3,2,1:T(4,128)S(1)} %reshape.322), channel_id=1, replica_groups=mesh['gx'=16,'gy'=8] {'gx','gy'}, use_global_device_ids=true, to_apply=%region_4.7 | all-reduce | flops 1728 | bytes 13824 | tf_op jit(solution)/shard_map/psum | solution.py:193
  474.6 77.1 %all-reduce.5.cloned.1.call-done = (f32[256,64]{0,1:T(8,128)}, f32[64,256]{1,0:T(8,128)}, f32[128,64,2,2,2]{0,1,4,3,2:T(8,128)}) async-done(((f32[256,64]{0,1:T(8,128)}, f32[64,256]{1,0:T(8,128)}, f32[128,64,2,2,2]{0,1,4,3,2:T(8,128)}), (f32[256,64]{0,1:T(8,128)}, f32[64,256]{1,0:T(8,128)}, f32[128,64,2,2,2]{0,1,4,3,2:T(8,128)})) %all-reduce.5.cloned.1.call-update) | async-done | bytes 393232 | tf_op jit(solution)/shard_map/psum | solution.py:193
  588.7 11.9 %select_maximum_fusion = bf16[8,64,4,10,130]{1,0,4,3,2:T(8,128)(2,1)} fusion(bf16[8,64,4,1,128]{1,0,4,3,2:T(8,128)(2,1)S(1)} %copy.136, bf16[8,64,4,1,128]{1,0,4,3,2:T(8,128)(2,1)} %copy.135, bf16[8,64,1,8,128]{1,0,4,3,2:T(8,128)(2,1)S(1)} %copy.132, bf16[8,64,2,8,128]{1,0,4,3,2:T(8,128)(2,1)} %bitcast.470, bf16[8,64,1,8,128]{1,0,4,3,2:T(8,128)(2,1)} %copy.131), kind=kLoop, calls=%fused_computation.95 | loop fusion | flops 47923200 | bytes 10567680 | tf_op jit(solution)/shard_map/concatenate | solution.py:20
  600.9 8.8 %maximum_maximum_fusion.1 = (bf16[8,64,4,9,128]{1,0,4,3,2:T(8,128)(2,1)}, bf16[8,64,4,9,128]{1,0,4,3,2:T(8,128)(2,1)}) fusion(bf16[8,64,1,8,128]{1,0,4,3,2:T(8,128)(2,1)S(1)} %copy.132, bf16[8,64,2,8,128]{1,0,4,3,2:T(8,128)(2,1)S(1)} %bitcast.474, bf16[8,64,1,8,128]{1,0,4,3,2:T(8,128)(2,1)S(1)} %copy-done.7, bf16[8,64,4,1,128]{1,0,4,3,2:T(8,128)(2,1)S(1)} %copy-done.12, ...), kind=kLoop, calls=%fused_computation.108 | loop fusion | flops 14155776 | bytes 14680064 | tf_op jit(solution)/shard_map/concatenate | solution.py:20
  610.0 39.6 %add_convert_fusion = bf16[8,64,2,8,128]{1,0,4,3,2:T(8,128)(2,1)} fusion(f32[8,64,2,8,128]{1,0,4,3,2:T(8,128)} %bitcast.475, bf16[8,64,2,8,128]{1,0,4,3,2:T(8,128)(2,1)} %bitcast.471, bf16[8,64,4,10,130]{1,0,4,3,2:T(8,128)(2,1)} %select_maximum_fusion, bf16[8,64,4,9,128]{1,0,4,3,2:T(8,128)(2,1)} %get-tuple-element.276, ...), kind=kLoop, calls=%fused_computation.136 | loop fusion | flops 88080384 | bytes 60824320 | tf_op jit(solution)/shard_map/convert_element_type | solution.py:170
  649.6 5.7 copy.144
  (327 shorter events, 253.8 us)
Async XLA Ops:
  7.2 544.6 %all-reduce.5.cloned.1.call-start = ((), (), s32[]{:S(2)}) async-start(), calls=%async_computation | async-start | bytes 786432 | tf_op jit(solution)/shard_map/psum | solution.py:193
  8.4 21.0 %collective-permute-start.13 = (bf16[1,128,4,4,64]{1,4,3,2,0:T(8,128)(2,1)S(1)}, bf16[1,128,4,4,64]{1,4,3,2,0:T(8,128)(2,1)S(1)}, u32[]{:S(2)}, u32[]{:S(2)}) collective-permute-start(bf16[1,128,4,4,64]{1,4,3,2,0:T(8,128)(2,1)S(1)} %get-tuple-element.292), channel_id=1, source_target_pairs={{1,0},{2,1},{3,2},{4,3},{5,4},{6,5},{7,6},{0,7},{9,8},{10,9},{11,1... | collective-permute-start | bytes 786440 | tf_op jit(solution)/shard_map/ppermute | solution.py:27
  13.3 16.1 %collective-permute-start.12 = (bf16[1,128,4,4,64]{1,4,3,2,0:T(8,128)(2,1)S(1)}, bf16[1,128,4,4,64]{1,4,3,2,0:T(8,128)(2,1)S(1)}, u32[]{:S(2)}, u32[]{:S(2)}) collective-permute-start(bf16[1,128,4,4,64]{1,4,3,2,0:T(8,128)(2,1)S(1)} %get-tuple-element.292), channel_id=1, source_target_pairs={{7,0},{0,1},{1,2},{2,3},{3,4},{4,5},{5,6},{6,7},{15,8},{8,9},{9,10... | collective-permute-start | bytes 786440 | tf_op jit(solution)/shard_map/ppermute | solution.py:27
  16.0 18.4 %collective-permute-start.1 = (bf16[8,64,1,8,128]{4,3,2,1,0:T(8,128)(2,1)S(1)}, bf16[8,64,1,8,128]{4,3,2,1,0:T(8,128)(2,1)}, u32[]{:S(2)}, u32[]{:S(2)}) collective-permute-start(bf16[8,64,1,8,128]{4,3,2,1,0:T(8,128)(2,1)S(1)} %get-tuple-element.285), channel_id=1, source_target_pairs={{8,0},{16,8},{24,16},{32,24},{40,32},{48,40},{56,48},{64,56},{72,6... | collective-permute-start | bytes 3145736 | tf_op jit(solution)/shard_map/ppermute | solution.py:19
  18.9 18.1 %collective-permute-start = (bf16[8,64,1,8,128]{4,3,2,1,0:T(8,128)(2,1)}, bf16[8,64,1,8,128]{4,3,2,1,0:T(8,128)(2,1)S(1)}, u32[]{:S(2)}, u32[]{:S(2)}) collective-permute-start(bf16[8,64,1,8,128]{4,3,2,1,0:T(8,128)(2,1)} %get-tuple-element.286), channel_id=1, source_target_pairs={{0,8},{8,16},{16,24},{24,32},{32,40},{40,48},{48,56},{56,64},{64,7... | collective-permute-start | bytes 3145736 | tf_op jit(solution)/shard_map/ppermute | solution.py:18
  31.1 29.7 %collective-permute-start.19 = (bf16[2,128,1,4,64]{1,4,3,0,2:T(8,128)(2,1)}, bf16[2,128,1,4,64]{1,4,3,0,2:T(8,128)(2,1)S(1)}, u32[]{:S(2)}, u32[]{:S(2)}) collective-permute-start(bf16[2,128,1,4,64]{1,4,3,0,2:T(8,128)(2,1)} %get-tuple-element.288), channel_id=1, source_target_pairs={{8,0},{16,8},{24,16},{32,24},{40,32},{48,40},{56,48},{64,56},{72,6... | collective-permute-start | bytes 393224 | tf_op jit(solution)/shard_map/ppermute | solution.py:27
  31.1 29.7 %collective-permute-start.18 = (bf16[2,128,1,4,64]{1,4,3,0,2:T(8,128)(2,1)}, bf16[2,128,1,4,64]{1,4,3,0,2:T(8,128)(2,1)S(1)}, u32[]{:S(2)}, u32[]{:S(2)}) collective-permute-start(bf16[2,128,1,4,64]{1,4,3,0,2:T(8,128)(2,1)} %get-tuple-element.288), channel_id=1, source_target_pairs={{104,0},{112,8},{120,16},{0,24},{8,32},{16,40},{24,48},{32,56},{40... | collective-permute-start | bytes 393224 | tf_op jit(solution)/shard_map/ppermute | solution.py:27
  46.7 33.7 %collective-permute-start.3 = (bf16[8,64,4,1,128]{4,1,3,2,0:T(8,128)(2,1)}, bf16[8,64,4,1,128]{4,1,3,2,0:T(8,128)(2,1)}, u32[]{:S(2)}, u32[]{:S(2)}) collective-permute-start(bf16[8,64,4,1,128]{4,1,3,2,0:T(8,128)(2,1)} %copy.102), channel_id=1, source_target_pairs={{1,0},{2,1},{3,2},{4,3},{5,4},{6,5},{7,6},{9,8},{10,9},{11,10},{12... | collective-permute-start | bytes 1572872 | tf_op jit(solution)/shard_map/ppermute | solution.py:19
  47.9 34.0 %collective-permute-start.2 = (bf16[8,64,4,1,128]{4,1,3,2,0:T(8,128)(2,1)}, bf16[8,64,4,1,128]{4,1,3,2,0:T(8,128)(2,1)}, u32[]{:S(2)}, u32[]{:S(2)}) collective-permute-start(bf16[8,64,4,1,128]{4,1,3,2,0:T(8,128)(2,1)} %copy.101), channel_id=1, source_target_pairs={{0,1},{1,2},{2,3},{3,4},{4,5},{5,6},{6,7},{8,9},{9,10},{10,11},{11... | collective-permute-start | bytes 1572872 | tf_op jit(solution)/shard_map/ppermute | solution.py:18
  57.5 11.4 %collective-permute-start.17 = (bf16[2,128,1,4,64]{1,4,3,0,2:T(8,128)(2,1)}, bf16[2,128,1,4,64]{1,4,3,0,2:T(8,128)(2,1)S(1)}, u32[]{:S(2)}, u32[]{:S(2)}) collective-permute-start(bf16[2,128,1,4,64]{1,4,3,0,2:T(8,128)(2,1)} %get-tuple-element.289), channel_id=1, source_target_pairs={{16,0},{24,8},{32,16},{40,24},{48,32},{56,40},{64,48},{72,56},{80,... | collective-permute-start | bytes 393224 | tf_op jit(solution)/shard_map/ppermute | solution.py:27
  60.8 18.9 %collective-permute-start.16 = (bf16[2,128,1,4,64]{1,4,3,0,2:T(8,128)(2,1)}, bf16[2,128,1,4,64]{1,4,3,0,2:T(8,128)(2,1)S(1)}, u32[]{:S(2)}, u32[]{:S(2)}) collective-permute-start(bf16[2,128,1,4,64]{1,4,3,0,2:T(8,128)(2,1)} %get-tuple-element.289), channel_id=1, source_target_pairs={{112,0},{120,8},{0,16},{8,24},{16,32},{24,40},{32,48},{40,56},{48,... | collective-permute-start | bytes 393224 | tf_op jit(solution)/shard_map/ppermute | solution.py:27
  61.5 132.9 %collective-permute-start.15 = (bf16[2,128,1,4,64]{1,4,3,0,2:T(8,128)(2,1)}, bf16[2,128,1,4,64]{1,4,3,0,2:T(8,128)(2,1)}, u32[]{:S(2)}, u32[]{:S(2)}) collective-permute-start(bf16[2,128,1,4,64]{1,4,3,0,2:T(8,128)(2,1)} %get-tuple-element.290), channel_id=1, source_target_pairs={{24,0},{32,8},{40,16},{48,24},{56,32},{64,40},{72,48},{80,56},{88,... | collective-permute-start | bytes 393224 | tf_op jit(solution)/shard_map/ppermute | solution.py:27
  68.9 125.5 %collective-permute-start.14 = (bf16[2,128,1,4,64]{1,4,3,0,2:T(8,128)(2,1)}, bf16[2,128,1,4,64]{1,4,3,0,2:T(8,128)(2,1)}, u32[]{:S(2)}, u32[]{:S(2)}) collective-permute-start(bf16[2,128,1,4,64]{1,4,3,0,2:T(8,128)(2,1)} %get-tuple-element.290), channel_id=1, source_target_pairs={{120,0},{0,8},{8,16},{16,24},{24,32},{32,40},{40,48},{48,56},{56,6... | collective-permute-start | bytes 393224 | tf_op jit(solution)/shard_map/ppermute | solution.py:27
  193.6 16.7 %collective-permute-start.9 = (bf16[2,128,1,4,64]{1,4,3,0,2:T(8,128)(2,1)}, bf16[2,128,1,4,64]{1,4,3,0,2:T(8,128)(2,1)}, u32[]{:S(2)}, u32[]{:S(2)}) collective-permute-start(bf16[2,128,1,4,64]{1,4,3,0,2:T(8,128)(2,1)} %get-tuple-element.296), channel_id=1, source_target_pairs={{8,0},{16,8},{24,16},{32,24},{40,32},{48,40},{56,48},{64,56},{72,6... | collective-permute-start | bytes 393224 | tf_op jit(solution)/shard_map/ppermute | solution.py:27
  194.1 17.2 %collective-permute-start.8 = (bf16[2,128,1,4,64]{1,4,3,0,2:T(8,128)(2,1)}, bf16[2,128,1,4,64]{1,4,3,0,2:T(8,128)(2,1)}, u32[]{:S(2)}, u32[]{:S(2)}) collective-permute-start(bf16[2,128,1,4,64]{1,4,3,0,2:T(8,128)(2,1)} %get-tuple-element.296), channel_id=1, source_target_pairs={{104,0},{112,8},{120,16},{0,24},{8,32},{16,40},{24,48},{32,56},{40... | collective-permute-start | bytes 393224 | tf_op jit(solution)/shard_map/ppermute | solution.py:27
  197.0 15.2 %collective-permute-start.7 = (bf16[2,128,1,4,64]{1,4,3,0,2:T(8,128)(2,1)}, bf16[2,128,1,4,64]{1,4,3,0,2:T(8,128)(2,1)S(1)}, u32[]{:S(2)}, u32[]{:S(2)}) collective-permute-start(bf16[2,128,1,4,64]{1,4,3,0,2:T(8,128)(2,1)} %get-tuple-element.297), channel_id=1, source_target_pairs={{16,0},{24,8},{32,16},{40,24},{48,32},{56,40},{64,48},{72,56},{80,... | collective-permute-start | bytes 393224 | tf_op jit(solution)/shard_map/ppermute | solution.py:27
  202.8 10.6 %collective-permute-start.6 = (bf16[2,128,1,4,64]{1,4,3,0,2:T(8,128)(2,1)}, bf16[2,128,1,4,64]{1,4,3,0,2:T(8,128)(2,1)S(1)}, u32[]{:S(2)}, u32[]{:S(2)}) collective-permute-start(bf16[2,128,1,4,64]{1,4,3,0,2:T(8,128)(2,1)} %get-tuple-element.297), channel_id=1, source_target_pairs={{112,0},{120,8},{0,16},{8,24},{16,32},{24,40},{32,48},{40,56},{48,... | collective-permute-start | bytes 393224 | tf_op jit(solution)/shard_map/ppermute | solution.py:27
  204.2 9.2 %collective-permute-start.5 = (bf16[2,128,1,4,64]{1,4,3,0,2:T(8,128)(2,1)}, bf16[2,128,1,4,64]{1,4,3,0,2:T(8,128)(2,1)S(1)}, u32[]{:S(2)}, u32[]{:S(2)}) collective-permute-start(bf16[2,128,1,4,64]{1,4,3,0,2:T(8,128)(2,1)} %get-tuple-element.298), channel_id=1, source_target_pairs={{24,0},{32,8},{40,16},{48,24},{56,32},{64,40},{72,48},{80,56},{88,... | collective-permute-start | bytes 393224 | tf_op jit(solution)/shard_map/ppermute | solution.py:27
  216.3 360.0 %collective-permute-start.11 = (bf16[1,128,4,4,64]{1,4,3,2,0:T(8,128)(2,1)}, bf16[1,128,4,4,64]{1,4,3,2,0:T(8,128)(2,1)}, u32[]{:S(2)}, u32[]{:S(2)}) collective-permute-start(bf16[1,128,4,4,64]{1,4,3,2,0:T(8,128)(2,1)} %get-tuple-element.294), channel_id=1, source_target_pairs={{1,0},{2,1},{3,2},{4,3},{5,4},{6,5},{7,6},{0,7},{9,8},{10,9},{11,1... | collective-permute-start | bytes 786440 | tf_op jit(solution)/shard_map/ppermute | solution.py:27
  216.9 359.4 %collective-permute-start.10 = (bf16[1,128,4,4,64]{1,4,3,2,0:T(8,128)(2,1)}, bf16[1,128,4,4,64]{1,4,3,2,0:T(8,128)(2,1)}, u32[]{:S(2)}, u32[]{:S(2)}) collective-permute-start(bf16[1,128,4,4,64]{1,4,3,2,0:T(8,128)(2,1)} %get-tuple-element.294), channel_id=1, source_target_pairs={{7,0},{0,1},{1,2},{2,3},{3,4},{4,5},{5,6},{6,7},{15,8},{8,9},{9,10... | collective-permute-start | bytes 786440 | tf_op jit(solution)/shard_map/ppermute | solution.py:27
  364.9 191.7 %collective-permute-start.21 = (bf16[8,64,1,8,128]{4,3,2,1,0:T(8,128)(2,1)}, bf16[8,64,1,8,128]{4,3,2,1,0:T(8,128)(2,1)}, u32[]{:S(2)}, u32[]{:S(2)}) collective-permute-start(bf16[8,64,1,8,128]{4,3,2,1,0:T(8,128)(2,1)} %copy.130), channel_id=1, source_target_pairs={{8,0},{16,8},{24,16},{32,24},{40,32},{48,40},{56,48},{64,56},{72,6... | collective-permute-start | bytes 3145736 | tf_op jit(solution)/shard_map/ppermute | solution.py:19
  372.7 186.6 %collective-permute-start.20 = (bf16[8,64,1,8,128]{4,3,2,1,0:T(8,128)(2,1)}, bf16[8,64,1,8,128]{4,3,2,1,0:T(8,128)(2,1)}, u32[]{:S(2)}, u32[]{:S(2)}) collective-permute-start(bf16[8,64,1,8,128]{4,3,2,1,0:T(8,128)(2,1)} %copy.129), channel_id=1, source_target_pairs={{0,8},{8,16},{16,24},{24,32},{32,40},{40,48},{48,56},{56,64},{64,7... | collective-permute-start | bytes 3145736 | tf_op jit(solution)/shard_map/ppermute | solution.py:18
  570.2 14.5 %collective-permute-start.23 = (bf16[8,64,4,1,128]{4,1,3,2,0:T(8,128)(2,1)}, bf16[8,64,4,1,128]{4,1,3,2,0:T(8,128)(2,1)}, u32[]{:S(2)}, u32[]{:S(2)}) collective-permute-start(bf16[8,64,4,1,128]{4,1,3,2,0:T(8,128)(2,1)} %copy.134), channel_id=1, source_target_pairs={{1,0},{2,1},{3,2},{4,3},{5,4},{6,5},{7,6},{9,8},{10,9},{11,10},{12... | collective-permute-start | bytes 1572872 | tf_op jit(solution)/shard_map/ppermute | solution.py:19
  571.5 14.8 %collective-permute-start.22 = (bf16[8,64,4,1,128]{4,1,3,2,0:T(8,128)(2,1)}, bf16[8,64,4,1,128]{4,1,3,2,0:T(8,128)(2,1)}, u32[]{:S(2)}, u32[]{:S(2)}) collective-permute-start(bf16[8,64,4,1,128]{4,1,3,2,0:T(8,128)(2,1)} %copy.133), channel_id=1, source_target_pairs={{0,1},{1,2},{2,3},{3,4},{4,5},{5,6},{6,7},{8,9},{9,10},{10,11},{11... | collective-permute-start | bytes 1572872 | tf_op jit(solution)/shard_map/ppermute | solution.py:18
  (79 other events, 1069.4 us)
Sparse Core Ops, SparseCore 0:
  401.1 150.6 all-reduce.4
where the time goes:
time: 672 us; the launch traced here: 662 us
  other arithmetic  189 us (28%)
  local copies, waits for them, and re-layouts  136 us (20%)
  matrix products  93.3 us (14%)
  waiting for transfers between devices  84.1 us (13%)
  blocking collectives  73 us (11%)
  starting transfers between devices  70.8 us (11%)
  between operations  15.7 us (2%)
    psum x1, waiting for transfers between devices, per_device(): lax.psum((grad_depthw, grad_inw, grad_outw, grad_downw.reshape(out_chans,...  77.1 us
    psum x1, blocking collectives, per_device(): lax.psum((grad_depthw, grad_inw, grad_outw, grad_downw.reshape(out_chans,...  73 us
    ppermute x16, starting transfers between devices, shifted(): return lax.ppermute(block, axis, route)  43 us
    concatenate x4, other arithmetic, padded_2(): x = jnp.concatenate([before, x, after], axis=dim)  41.5 us
    dot_general x3, other arithmetic, per_device(): lax.dot_general(grad_depth, window, (((0, 2, 3, 4), (0, 2, 3, 4)), ((1,),...  39.7 us
    convert_element_type x1, other arithmetic, per_device(): (grad_merged.reshape(fields.shape).astype(jnp.float32) + adjoint).astype(...  39.6 us
    convert_element_type x1, other arithmetic, per_device(): depth_conv(padded, depth_kernel, span_x, span_y, span_z)  37.4 us
    dot_general x8, matrix products, forward_one(): branch = jnp.dot(point_out, active, preferred_element_type=jnp.float32)  22.6 us
  transfers between devices with their start and end apart: 25, of which 4 were waited for; matrix products, arithmetic and copies ran while one was open for 52% of the time, Pallas kernels for 0%

commit v1 on v0

v1 whole, which is shorter than its diff:
```python
import math

import jax
import jax.numpy as jnp
from jax import lax
from jax.experimental import pallas as pl
from jax.experimental.pallas import tpu as pltpu
from jax.sharding import PartitionSpec as P

NGX, NGY = 16, 8
S, C, HID, C2 = 8, 64, 256, 128
F32, BF16 = jnp.float32, jnp.bfloat16
MESH = pl.DeviceIdType.MESH
NN = (((1,), (0,)), ((), ()))
NT = (((1,), (1,)), ((), ()))
TN = (((0,), (0,)), ((), ()))
G0 = math.sqrt(2.0 / math.pi)
G1 = G0 * 0.044715
ROWS = 384 // NGX
SCALE = 1.0 / math.sqrt(8 * 32 * 64 * 128)


def dot(a, b, dims=NN):
    return lax.dot_general(a, b, dims, preferred_element_type=F32)


def taps(grid, s, j, g):
    sides = []
    for yy in range(2):
        block = grid[s, :, pl.ds(2 * j + yy, 3), 16 * g : 16 * g + 16, :]
        sides.append(block.reshape(192, 128))
    return jnp.concatenate(sides, axis=1)


def shifted_sum(a0, a1, a2):
    lane = lax.broadcasted_iota(jnp.int32, a1.shape, 1)
    low = lane < 64
    near = pltpu.roll(jnp.where(low, a0, a2), 64, 1)
    far = jnp.where(low, pltpu.roll(a0, 65, 1), pltpu.roll(a2, 63, 1))
    return a1 + near + jnp.where((lane == 0) | (lane == 127), 0.0, far)


def conv(grid, mats, s, j):
    parts = [dot(mats[g], taps(grid, s, j, g)) for g in range(4)]
    result = []
    for x in range(2):
        sides = []
        for yy in range(2):
            a = [
                jnp.concatenate(
                    [p[48 * x + 16 * e : 48 * x + 16 * e + 16, 128 * yy : 128 * yy + 128] for p in parts],
                    axis=0,
                )
                for e in range(3)
            ]
            sides.append(shifted_sum(*a))
        result.append(jnp.concatenate(sides, axis=1))
    return result


def kernel(
    raw, cot, lanes, pin, pin_t, pout, pout_t, w2t,
    coarse, grad_out, sums_out, dw_out,
    fg, dg, gm, gdn, red, mats, mats_t, wacc, dwacc, swap, rs, gyb, tot, t1, t2,
    f_send, f_recv, d_send, d_recv, c_send, c_recv, r_send, r_recv,
    rs_send, rs_recv, gy_send, gy_recv, ag_send, ag_recv, t1_send, t1_recv, t2_send, t2_recv, own_sem,
):
    ix, iy = lax.axis_index("gx"), lax.axis_index("gy")
    mx, my = ix % 4, iy % 2
    mine = mx * 2 + my
    bx, by = ix - mx, iy - my

    zero = jnp.zeros((S, 10, C, 128), BF16)
    zero_y = jnp.zeros((S, 4, C, 128), BF16)
    for grid in (fg, dg):
        for cond, at in ((ix == 0, 0), (ix == NGX - 1, 3)):

            @pl.when(cond)
            def _(grid=grid, at=at):
                @pl.loop(0, S)
                def _(s):
                    grid[s, at] = jnp.zeros((10, C, 128), BF16)

        for cond, at in ((iy == 0, 0), (iy == NGY - 1, 9)):

            @pl.when(cond)
            def _(grid=grid, at=at):
                @pl.loop(0, S)
                def _(s):
                    grid[s, :, at] = jnp.zeros((4, C, 128), BF16)

    barrier = pltpu.get_barrier_semaphore()
    peers = [((ix + k) % NGX, iy) for k in range(1, NGX)]
    peers += [(ix, (iy + k) % NGY) for k in range(1, NGY)]
    peers += [((ix + p) % NGX, (iy + q) % NGY) for p in (1, NGX - 1) for q in (1, NGY - 1)]
    peers += [(bx + (mx + k) % 4, by + 1 - my) for k in range(1, 4)]
    for peer in peers:
        pl.semaphore_signal(barrier, inc=1, device_id=peer, device_id_type=MESH)
    pl.semaphore_wait(barrier, len(peers))

    def remote(src, dst, send, recv, to):
        return pltpu.make_async_remote_copy(
            src_ref=src, dst_ref=dst, send_sem=send, recv_sem=recv, device_id=to, device_id_type=MESH
        )

    def cot_copy(k):
        to = (mine + k) % 8
        tx, ty = to // 2, to % 2
        return remote(
            cot.at[tx, pl.ds(ty * 4, 4)], gdn.at[mine], c_send.at[to], c_recv.at[mine], (bx + tx, by + ty)
        )

    def cot_arrival(s):
        return remote(cot.at[0, pl.ds(0, 4)], gdn.at[s], c_send.at[s], c_recv.at[s], (ix, iy))

    for k in range(1, 8):
        cot_copy(k).start()
    gdn[mine] = cot[mx, pl.ds(my * 4, 4)]

    row = lax.broadcasted_iota(jnp.int32, (16, 192), 0)
    col = lax.broadcasted_iota(jnp.int32, (16, 192), 1)
    diag = row == col % 16
    for m, (to, base) in enumerate(((mats, 0), (mats_t, 24))):
        for g in range(4):
            for q in range(6):
                line = lanes[base + 6 * g + q : base + 6 * g + q + 1, :]
                to[g, 16 * q : 16 * q + 16] = jnp.where(diag, line, 0.0).astype(BF16)
    wacc[...] = jnp.zeros_like(wacc)
    dwacc[...] = jnp.zeros_like(dwacc)

    zi = lax.broadcasted_iota(jnp.int32, (128, 128), 0)
    li = lax.broadcasted_iota(jnp.int32, (128, 128), 1)
    perm = (zi == jnp.where(li < 64, 2 * li, 2 * li - 127)).astype(BF16)

    def rims(grid, s, send, recv):
        whole, inner = pl.ds(1, 8), pl.ds(1, 2)
        west, east, south, north = ix > 0, ix < NGX - 1, iy > 0, iy < NGY - 1
        listed = [
            (west, east, (ix - 1, iy), (1, whole), (3, whole)),
            (east, west, (ix + 1, iy), (2, whole), (0, whole)),
            (south, north, (ix, iy - 1), (inner, 1), (inner, 9)),
            (north, south, (ix, iy + 1), (inner, 8), (inner, 0)),
            (west & south, east & north, (ix - 1, iy - 1), (1, 1), (3, 9)),
            (west & north, east & south, (ix - 1, iy + 1), (1, 8), (3, 0)),
            (east & south, west & north, (ix + 1, iy - 1), (2, 1), (0, 9)),
            (east & north, west & south, (ix + 1, iy + 1), (2, 8), (0, 0)),
        ]
        return [
            (goes, comes, remote(grid.at[(s, *src)], grid.at[(s, *dst)], send.at[s, d], recv.at[s, d], to))
            for d, (goes, comes, to, src, dst) in enumerate(listed)
        ]

    def send_rims(grid, s, send, recv):
        for goes, _, copy in rims(grid, s, send, recv):
            pl.when(goes)(copy.start)

    def await_rims(grid, s, send, recv):
        for _, comes, copy in rims(grid, s, send, recv):
            pl.when(comes)(copy.wait_recv)

    @pl.loop(0, S)
    def _(s):
        for h in range(4):
            block = raw[s, 16 * h : 16 * h + 16].reshape(256, 128)
            turned = dot(block, perm).reshape(16, 16, 128)
            turned = jnp.swapaxes(turned, 0, 1).astype(BF16)
            for x in range(2):
                fg[s, 1 + x, 1:9, 16 * h : 16 * h + 16, :] = turned[8 * x : 8 * x + 8]
        send_rims(fg, s, f_send, f_recv)

    def coarse_copy(s):
        return remote(
            red.at[s], coarse.at[mx, pl.ds(my * 4, 4)], r_send.at[s], r_recv.at[mine], (bx + s // 2, by + s % 2)
        )

    def coarse_arrival(s):
        return remote(
            red.at[s], coarse.at[s // 2, pl.ds(s % 2 * 4, 4)], r_send.at[s], r_recv.at[s], (ix, iy)
        )

    def own_coarse():
        return pltpu.make_async_copy(red.at[mine], coarse.at[mx, pl.ds(my * 4, 4)], own_sem)

    @pl.loop(0, S)
    def _(s):
        await_rims(fg, s, f_send, f_recv)

        @pl.when(s != mine)
        def _():
            cot_arrival(s).wait_recv()

        @pl.loop(0, 4)
        def _(j):
            down = gdn[s, j]
            none = jnp.zeros_like(down)
            down = jnp.concatenate(
                [jnp.concatenate([down, none], axis=1), jnp.concatenate([none, down], axis=1)], axis=0
            )
            gm_all = dot(w2t[...], down, NT).astype(BF16)
            depth = conv(fg, mats, s, j)
            stacked = []
            for x in range(2):
                dep = depth[x].astype(BF16)
                gm_x = jnp.concatenate(
                    [gm_all[128 * x : 128 * x + 64], gm_all[128 * x + 64 : 128 * x + 128]], axis=1
                )
                pre = dot(pin[...], dep)
                sq = pre * pre
                t = jnp.tanh(pre * (G0 + G1 * sq))
                half = 0.5 * pre
                act = (half + half * t).astype(BF16)
                own = jnp.concatenate(
                    [fg[s, 1 + x, 1 + 2 * j + yy].astype(F32) for yy in range(2)], axis=1
                )
                merged = (own + dot(pout[...], act)).astype(BF16)
                stacked += [merged[:, :128], merged[:, 128:]]
                slope = 0.5 + 0.5 * t + half * (1.0 - t * t) * (G0 + 3 * G1 * sq)
                gpre = (dot(pout_t[...], gm_x) * slope).astype(BF16)
                wacc[0:64] += dot(gm_x, act, NT)
                wacc[64:128] += dot(dep, gpre, NT)
                gdep = dot(pin_t[...], gpre).astype(BF16)
                for yy in range(2):
                    dg[s, 1 + x, 1 + 2 * j + yy] = gdep[:, 128 * yy : 128 * yy + 128]
                    gm[s, x, 2 * j + yy] = gm_x[:, 128 * yy : 128 * yy + 128]
            stacked = jnp.concatenate(stacked, axis=0)
            wacc[128:384] += dot(stacked, down)
            both = dot(stacked, w2t[...], TN)
            red[s, j] = (both[:64, :128] + both[64:, 128:]).astype(BF16)

        send_rims(dg, s, d_send, d_recv)

        @pl.when(s != mine)
        def _():
            coarse_copy(s).start()

    own_coarse().start()

    def rs_copy(k):
        to = (ix + k) % NGX
        return remote(wacc.at[pl.ds(to * ROWS, ROWS)], rs.at[ix], rs_send.at[k], rs_recv.at[NGX - k], (to, iy))

    def gy_copy(k):
        to = (iy + k) % NGY
        return remote(gyb.at[iy], gyb.at[iy], gy_send.at[k], gy_recv.at[NGY - k], (ix, to))

    def ag_copy(k):
        to = (ix + k) % NGX
        return remote(tot.at[ix], tot.at[ix], ag_send.at[k], ag_recv.at[NGX - k], (to, iy))

    def t1_copy(k):
        to = (ix + k) % NGX
        return remote(t1.at[ix], t1.at[ix], t1_send.at[k], t1_recv.at[NGX - k], (to, iy))

    def t2_copy(k):
        to = (iy + k) % NGY
        return remote(t2.at[iy], t2.at[iy], t2_send.at[k], t2_recv.at[NGY - k], (ix, to))

    def arrival(buffer, slot, send, recv, k):
        return remote(buffer.at[slot], buffer.at[slot], send.at[k], recv.at[k], (ix, iy))

    def total(buffer, n):
        result = buffer[0]
        for q in range(1, n):
            result = result + buffer[q]
        return result

    for k in range(1, NGX):
        rs_copy(k).start()
    rs[ix] = wacc[pl.ds(pl.multiple_of(ix * ROWS, 8), ROWS)]

    @pl.loop(0, S)
    def _(s):
        await_rims(dg, s, d_send, d_recv)

        @pl.loop(0, 4)
        def _(j):
            adjoint = conv(dg, mats_t, s, j)
            lefts = []
            for x in range(2):
                sides = []
                for yy in range(2):
                    at = 2 * j + yy
                    summed = gm[s, x, at].astype(F32) + adjoint[x][:, 128 * yy : 128 * yy + 128]
                    back = dot(summed.astype(BF16), perm, NT)
                    swap[8 * x + at] = back
                    here = dg[s, 1 + x, 1 + at].astype(F32)
                    none = jnp.zeros_like(here)
                    sides.append((shifted_sum(none, none, here), here, shifted_sum(here, none, none)))
                for e in range(3):
                    lefts.append(jnp.concatenate([sides[0][e], sides[1][e]], axis=1).astype(BF16))
            for g in range(4):
                left = jnp.concatenate([m[16 * g : 16 * g + 16] for m in lefts], axis=0)
                dwacc[g] += dot(left, taps(fg, s, j, g), NT)

        for h in range(4):
            turned = jnp.swapaxes(swap[:, 16 * h : 16 * h + 16, :], 0, 1)
            grad_out[s, 16 * h : 16 * h + 16] = turned.astype(BF16)

        @pl.when(s == 2)
        def _():
            for k in range(1, NGX):
                arrival(rs, (ix + k) % NGX, rs_send, rs_recv, k).wait_recv()
            gyb[iy] = total(rs, NGX)
            for k in range(1, NGY):
                gy_copy(k).start()

        @pl.when(s == 5)
        def _():
            for k in range(1, NGY):
                arrival(gyb, (iy + k) % NGY, gy_send, gy_recv, k).wait_recv()
            tot[ix] = total(gyb, NGY) * SCALE
            for k in range(1, NGX):
                ag_copy(k).start()

    lines = []
    for g in range(4):
        for q in range(6):
            block = jnp.where(diag, dwacc[g, 16 * q : 16 * q + 16, :], 0.0)
            lines.append(jnp.sum(block, axis=0, keepdims=True))
    t1[ix] = jnp.concatenate(lines, axis=0)
    for k in range(1, NGX):
        t1_copy(k).start()
    for k in range(1, NGX):
        arrival(t1, (ix + k) % NGX, t1_send, t1_recv, k).wait_recv()
    t2[iy] = total(t1, NGX)
    for k in range(1, NGY):
        t2_copy(k).start()
    for k in range(1, NGX):
        arrival(tot, (ix + k) % NGX, ag_send, ag_recv, k).wait_recv()
    sums_out[...] = tot[...]
    for k in range(1, NGY):
        arrival(t2, (iy + k) % NGY, t2_send, t2_recv, k).wait_recv()
    dw_out[...] = total(t2, NGY) * SCALE

    own_coarse().wait()

    @pl.loop(0, S)
    def _(s):
        @pl.when(s != mine)
        def _():
            coarse_arrival(s).wait_recv()
            coarse_copy(s).wait_send()

        for grid, send, recv in ((fg, f_send, f_recv), (dg, d_send, d_recv)):
            for goes, _, copy in rims(grid, s, send, recv):
                pl.when(goes)(copy.wait_send)

    for k in range(1, 8):
        cot_copy(k).wait_send()
    for k in range(1, NGX):
        rs_copy(k).wait_send()
        ag_copy(k).wait_send()
        t1_copy(k).wait_send()
    for k in range(1, NGY):
        gy_copy(k).wait_send()
        t2_copy(k).wait_send()


def per_device(fields, depth_kernel, point_in, point_out, down_kernel, cotangent):
    raw = fields.reshape(S, C, 16, 128)
    cot = cotangent[0, 0, 0].transpose(1, 2, 3, 0)
    w = depth_kernel.astype(F32).transpose(1, 2, 3, 0)
    w = jnp.stack([w, w[::-1, ::-1, ::-1]])
    w = jnp.stack([jnp.pad(w, ((0, 0), (x, 1 - x), (0, 0), (0, 0), (0, 0))) for x in range(2)])
    lanes = w.reshape(2, 2, 4, 3, 3, 4, 16).transpose(1, 5, 0, 4, 2, 3, 6).reshape(48, 192)
    w2t = down_kernel.transpose(2, 3, 1, 4, 0).reshape(256, 256)
    vmem = pl.BlockSpec(memory_space=pltpu.VMEM)
    dma = pltpu.SemaphoreType.DMA
    coarse, grad, sums, dw = pl.pallas_call(
        kernel,
        out_shape=(
            jax.ShapeDtypeStruct((4, 8, 64, 128), BF16),
            jax.ShapeDtypeStruct((S, C, 16, 128), BF16),
            jax.ShapeDtypeStruct((NGX, ROWS, 256), F32),
            jax.ShapeDtypeStruct((24, 192), F32),
        ),
        in_specs=[vmem] * 8,
        out_specs=[vmem] * 4,
        scratch_shapes=[
            pltpu.VMEM((S, 4, 10, C, 128), BF16),
            pltpu.VMEM((S, 4, 10, C, 128), BF16),
            pltpu.VMEM((S, 2, 8, C, 128), BF16),
            pltpu.VMEM((S, 4, 64, 128), BF16),
            pltpu.VMEM((S, 4, 64, 128), BF16),
            pltpu.VMEM((4, 96, 192), BF16),
            pltpu.VMEM((4, 96, 192), BF16),
            pltpu.VMEM((384, 256), F32),
            pltpu.VMEM((4, 96, 192), F32),
            pltpu.VMEM((16, C, 128), F32),
            pltpu.VMEM((NGX, ROWS, 256), F32),
            pltpu.VMEM((NGY, ROWS, 256), F32),
            pltpu.VMEM((NGX, ROWS, 256), F32),
            pltpu.VMEM((NGX, 24, 192), F32),
            pltpu.VMEM((NGY, 24, 192), F32),
            dma((S, 8)), dma((S, 8)), dma((S, 8)), dma((S, 8)),
            dma((8,)), dma((8,)), dma((8,)), dma((8,)),
            dma((NGX,)), dma((NGX,)), dma((NGY,)), dma((NGY,)), dma((NGX,)), dma((NGX,)),
            dma((NGX,)), dma((NGX,)), dma((NGY,)), dma((NGY,)),
            dma,
        ],
        compiler_params=pltpu.CompilerParams(
            collective_id=0, has_side_effects=True, vmem_limit_bytes=56 * 2**20
        ),
    )(raw, cot, lanes, point_in, point_in.T, point_out, point_out.T, w2t)
    coarse = coarse.transpose(3, 0, 1, 2)[None, None, None]
    sums = sums.reshape(384, 256)
    grad_down = sums[128:].reshape(2, 2, 64, 2, 128).transpose(4, 2, 0, 1, 3)
    dw = dw.reshape(4, 2, 3, 4, 3, 16)
    dw = dw[:, 0, :, :3] + dw[:, 1, :, 1:]
    dw = dw.transpose(0, 4, 2, 3, 1).reshape(C, 3, 3, 3)
    return coarse, grad.reshape(fields.shape), dw, sums[64:128].T, sums[:64], grad_down


def solution(mesh):
    split = P("gx", "gy", None, None, None, None, None)
    fine = P(None, None, "gx", "gy", None)
    return jax.shard_map(
        per_device,
        mesh=mesh,
        in_specs=(fine, P(), P(), P(), P(), split),
        out_specs=(split, fine, P(), P(), P(), P()),
        check_vma=False,
    )
```

time: 672 us -> 123 us (0.18); the launches traced: 662 us -> 122 us
  other arithmetic: 189 us -> 0.82 us
  local copies, waits for them, and re-layouts: 136 us -> 14.4 us
  Pallas kernels: 0 us -> 106 us
  matrix products: 93.3 us -> 0 us
  waiting for transfers between devices: 84.1 us -> 0 us
  blocking collectives: 73 us -> 0 us
  starting transfers between devices: 70.8 us -> 0 us
  between operations: 15.7 us -> 0.74 us
    pallas_call x0 -> x1, Pallas kernels: none -> 106 us  [per_device(): pl.pallas_call(kernel, out_shape=(jax.ShapeDtypeStruct((4, 8, 64, 128), B...]
    dot_general x51 -> x0, matrix products: 93.3 us -> none  [the longest x8 22.6 us: forward_one(): branch = jnp.dot(point_out, active, preferred_element_type=jnp.float32)]
    convert_element_type x5 -> x0, other arithmetic: 83.9 us -> none  [the longest x1 39.6 us: per_device(): (grad_merged.reshape(fields.shape).astype(jnp.float32) + adjoint).astype(...]
    psum x1 -> x0, waiting for transfers between devices: 77.1 us -> none  [per_device(): lax.psum((grad_depthw, grad_inw, grad_outw, grad_downw.reshape(out_chans,...]
    psum x1 -> x0, blocking collectives: 73 us -> none  [per_device(): lax.psum((grad_depthw, grad_inw, grad_outw, grad_downw.reshape(out_chans,...]
    ppermute x24 -> x0, starting transfers between devices: 70.7 us -> none  [the longest x16 43 us: shifted(): return lax.ppermute(block, axis, route)]
    concatenate x4 -> x0, other arithmetic: 41.5 us -> none  [padded_2(): x = jnp.concatenate([before, x, after], axis=dim)]
    dot_general x3 -> x0, other arithmetic: 39.7 us -> none  [per_device(): lax.dot_general(grad_depth, window, (((0, 2, 3, 4), (0, 2, 3, 4)), ((1,),...]
  transfers between devices with their start and end apart: 25 -> 0, of which waited for: 4 -> 0; matrix products, arithmetic and copies ran while one was open for 52% -> 0% of each run, Pallas kernels for 0% -> 0%
where the time goes in v1:
time: 123 us; the launch traced here: 122 us
  Pallas kernels  106 us (86%)
  local copies, waits for them, and re-layouts  14.4 us (12%)
    pallas_call x1, Pallas kernels, per_device(): pl.pallas_call(kernel, out_shape=(jax.ShapeDtypeStruct((4, 8, 64, 128), B...  106 us
    unnamed x9, local copies, waits for them, and re-layouts  7.65 us

profile of v1, /device:TPU:1, one launch (start us, length us, event | category | flops | bytes accessed | tf_op | source)
XLA Modules:
  0.0 122.4 jit_solution(12949543595226217047)
XLA Ops:
  0.6 0.7 convert_bitcast_fusion
  1.4 1.5 %copy.30.pin = bf16[256,64]{1,0:T(8,128)(2,1)} copy(bf16[256,64]{0,1:T(8,128)(2,1)} %param.8) | data formatting | bytes 65536 | tf_op args[2]
  2.9 1.5 %copy.28 = bf16[64,256]{0,1:T(8,128)(2,1)} copy(bf16[64,256]{1,0:T(8,128)(2,1)} %pout.1) | data formatting | bytes 65536 | tf_op args[3]
  4.4 0.1 stack.21
  4.6 1.0 copy.29
  5.6 0.7 copy.37
  6.2 0.1 stack.22
  6.4 0.1 maximum_bitcast_fusion
  6.5 0.2 copy.27
  6.6 0.9 reshape.43.lanes
  7.5 106.4 %shard_map.109 = (bf16[4,8,64,128]{3,2,1,0:T(8,128)(2,1)}, bf16[8,64,16,128]{3,2,1,0:T(8,128)(2,1)}, f32[16,24,256]{2,1,0:T(8,128)}, f32[24,192]{1,0:T(8,128)}) custom-call(bf16[8,64,16,128]{3,2,1,0:T(8,128)(2,1)} %bitcast.38, bf16[4,8,64,128]{3,2,1,0:T(8,128)(2,1)} %bitcast.44, f32[48,192]{1,0:T(8,128)} %reshape.43.lanes, bf16[256,64]{1,0:T(8,128)(2,1)} %copy.30.pin, ...), custom_call_target="tpu_custom_call" | custom-call | tf_op jit(solution)/shard_map/pallas_call | solution.py:369
  113.9 0.0 copy-start
  113.9 1.7 %fusion.1 = (f32[64,256]{1,0:T(8,128)}, f32[256,64]{0,1:T(8,128)}) fusion(f32[384,256]{1,0:T(8,128)} %bitcast.45), kind=kLoop, calls=%fused_computation.8 | loop fusion | bytes 262144 | tf_op jit(solution)/shard_map/slice | solution.py:411
  115.6 1.0 slice.24
  116.6 0.1 reshape.49
  116.7 0.8 copy.32
  117.5 0.9 reshape.46
  118.5 0.7 reshape.47
  119.2 1.9 %copy.40 = bf16[1,1,1,128,4,8,64]{3,6,5,4,2,1,0:T(8,128)(2,1)} copy(bf16[1,1,1,128,4,8,64]{3,6,5,4,2,1,0:T(8,128)(2,1)} %bitcast.42) | data formatting | bytes 1048576
  121.1 0.0 copy-done
  121.1 1.3 %copy.41 = bf16[8,64,2,8,128]{4,3,2,1,0:T(8,128)(2,1)} copy(bf16[8,64,2,8,128]{4,3,2,1,0:T(8,128)(2,1)S(1)} %bitcast.39) | data formatting | bytes 4194304
  (6 shorter events, 0.1 us)
Async XLA Ops:
  113.9 7.1 %copy-start = (bf16[8,64,16,128]{3,2,1,0:T(8,128)(2,1)S(1)}, bf16[8,64,16,128]{3,2,1,0:T(8,128)(2,1)}, u32[]{:S(2)}) copy-start(bf16[8,64,16,128]{3,2,1,0:T(8,128)(2,1)} %get-tuple-element.11) | copy-start | bytes 6291460

commit v2 on v1

v2 whole, which is shorter than its diff:
```python
import math

import jax
import jax.numpy as jnp
from jax import lax
from jax.experimental import pallas as pl
from jax.experimental.pallas import tpu as pltpu
from jax.sharding import PartitionSpec as P

NGX, NGY = 16, 8
S, C, HID, C2 = 8, 64, 256, 128
F32, BF16 = jnp.float32, jnp.bfloat16
MESH = pl.DeviceIdType.MESH
NN = (((1,), (0,)), ((), ()))
NT = (((1,), (1,)), ((), ()))
TN = (((0,), (0,)), ((), ()))
G0 = math.sqrt(2.0 / math.pi)
G1 = G0 * 0.044715
HALF, PART = 448, 56
SCALE = 1.0 / math.sqrt(8 * 32 * 64 * 128)


def dot(a, b, dims=NN):
    return lax.dot_general(a, b, dims, preferred_element_type=F32)


def taps(grid, s, j, g):
    sides = []
    for yy in range(2):
        block = grid[s, :, pl.ds(2 * j + yy, 3), 16 * g : 16 * g + 16, :]
        sides.append(block.reshape(192, 128))
    return jnp.concatenate(sides, axis=1)


def shifted_sum(a0, a1, a2):
    lane = lax.broadcasted_iota(jnp.int32, a1.shape, 1)
    low = lane < 64
    near = pltpu.roll(jnp.where(low, a0, a2), 64, 1)
    far = jnp.where(low, pltpu.roll(a0, 65, 1), pltpu.roll(a2, 63, 1))
    return a1 + near + jnp.where((lane == 0) | (lane == 127), 0.0, far)


def conv(grid, mats, s, j):
    parts = [dot(mats[g], taps(grid, s, j, g)) for g in range(4)]
    result = []
    for x in range(2):
        sides = []
        for yy in range(2):
            a = [
                jnp.concatenate(
                    [p[48 * x + 16 * e : 48 * x + 16 * e + 16, 128 * yy : 128 * yy + 128] for p in parts],
                    axis=0,
                )
                for e in range(3)
            ]
            sides.append(shifted_sum(*a))
        result.append(jnp.concatenate(sides, axis=1))
    return result


def kernel(
    raw_hbm, cot, taps_in, pin_t, pout, down_in,
    coarse, grad_out, grad_in, grad_po, grad_down, dw_out,
    raw, pin, pout_t, w2t, wide,
    fg, dg, gm, gdn, red, mats, mats_t, wacc, dwacc, swap, pair, rs, gyb, tot,
    f_send, f_recv, d_send, d_recv, c_send, c_recv, r_send, r_recv,
    rs_send, rs_recv, gy_send, gy_recv, ag_send, ag_recv, pair_send, pair_recv, own_sem, in_sem,
):
    ix, iy = lax.axis_index("gx"), lax.axis_index("gy")
    mx, my = ix % 4, iy % 2
    mine = mx * 2 + my
    bx, by = ix - mx, iy - my

    def load(s):
        return pltpu.make_async_copy(raw_hbm.at[s], raw.at[s], in_sem.at[s])

    for s in range(S):
        load(s).start()

    for grid in (fg, dg):
        for cond, at in ((ix == 0, 0), (ix == NGX - 1, 3)):

            @pl.when(cond)
            def _(grid=grid, at=at):
                @pl.loop(0, S)
                def _(s):
                    grid[s, at] = jnp.zeros((10, C, 128), BF16)

        for cond, at in ((iy == 0, 0), (iy == NGY - 1, 9)):

            @pl.when(cond)
            def _(grid=grid, at=at):
                @pl.loop(0, S)
                def _(s):
                    grid[s, :, at] = jnp.zeros((4, C, 128), BF16)

    barrier = pltpu.get_barrier_semaphore()
    core, chip = ix % 2, ix // 2
    peers = [((ix + k) % NGX, iy) for k in range(2, NGX, 2)]
    peers += [(ix + 1 - 2 * core, iy), ((ix + NGX - 1 + 2 * core) % NGX, iy)]
    peers += [(ix, (iy + k) % NGY) for k in range(1, NGY)]
    peers += [((ix + p) % NGX, (iy + q) % NGY) for p in (1, NGX - 1) for q in (1, NGY - 1)]
    peers += [(bx + (mine + k) % 8 // 2, by + (mine + k) % 2) for k in range(1, 8)]
    for peer in peers:
        pl.semaphore_signal(barrier, inc=1, device_id=peer, device_id_type=MESH)

    def remote(src, dst, send, recv, to):
        return pltpu.make_async_remote_copy(
            src_ref=src, dst_ref=dst, send_sem=send, recv_sem=recv, device_id=to, device_id_type=MESH
        )

    def cot_copy(k):
        to = (mine + k) % 8
        tx, ty = to // 2, to % 2
        return remote(
            cot.at[tx, pl.ds(ty * 4, 4)], gdn.at[mine], c_send.at[to], c_recv.at[mine], (bx + tx, by + ty)
        )

    def cot_arrival(s):
        return remote(cot.at[0, pl.ds(0, 4)], gdn.at[s], c_send.at[s], c_recv.at[s], (ix, iy))

    def send_cot():
        for k in range(1, 8):
            cot_copy(k).start()

    gdn[mine] = cot[mx, pl.ds(my * 4, 4)]

    pin[...] = pin_t[...].astype(F32).T.astype(BF16)
    pout_t[...] = pout[...].astype(F32).T.astype(BF16)
    wide[...] = down_in[...].astype(F32)
    for k in range(8):
        at = 64 * (k // 2)
        w2t[at : at + 64, k % 2 * 128 : k % 2 * 128 + 128] = wide[pl.ds(k, 64, stride=8), :].astype(BF16)

    row = lax.broadcasted_iota(jnp.int32, (16, 192), 0)
    col = lax.broadcasted_iota(jnp.int32, (16, 192), 1)
    diag = row == col % 16
    tap = lax.broadcasted_iota(jnp.int32, (27, 192), 0)
    spot = lax.broadcasted_iota(jnp.int32, (27, 192), 1)
    coefficients = taps_in[...]
    for q in range(6):
        x, e = q // 3, q % 3
        a = spot // 48 - x
        at = 9 * a + 3 * (spot // 16 % 3) + e
        inside = (a >= 0) & (a <= 2)
        for to, place in ((mats, at), (mats_t, 26 - at)):
            spread = dot(coefficients, ((tap == place) & inside).astype(BF16), TN)
            for g in range(4):
                to[g, 16 * q : 16 * q + 16] = jnp.where(diag, spread[16 * g : 16 * g + 16], 0.0).astype(BF16)
    wacc[...] = jnp.zeros_like(wacc)
    dwacc[...] = jnp.zeros_like(dwacc)

    zi = lax.broadcasted_iota(jnp.int32, (128, 128), 0)
    li = lax.broadcasted_iota(jnp.int32, (128, 128), 1)
    perm = (zi == jnp.where(li < 64, 2 * li, 2 * li - 127)).astype(BF16)

    def add(at, term):
        n = term.shape[0]
        wacc[at : at + n] += term[:, :128]
        wacc[at + n : at + 2 * n] += term[:, 128:]

    def rims(grid, s, send, recv):
        whole, inner = pl.ds(1, 8), pl.ds(1, 2)
        west, east, south, north = ix > 0, ix < NGX - 1, iy > 0, iy < NGY - 1
        listed = [
            (west, east, (ix - 1, iy), (1, whole), (3, whole)),
            (east, west, (ix + 1, iy), (2, whole), (0, whole)),
            (south, north, (ix, iy - 1), (inner, 1), (inner, 9)),
            (north, south, (ix, iy + 1), (inner, 8), (inner, 0)),
            (west & south, east & north, (ix - 1, iy - 1), (1, 1), (3, 9)),
            (west & north, east & south, (ix - 1, iy + 1), (1, 8), (3, 0)),
            (east & south, west & north, (ix + 1, iy - 1), (2, 1), (0, 9)),
            (east & north, west & south, (ix + 1, iy + 1), (2, 8), (0, 0)),
        ]
        return [
            (goes, comes, remote(grid.at[(s, *src)], grid.at[(s, *dst)], send.at[s, d], recv.at[s, d], to))
            for d, (goes, comes, to, src, dst) in enumerate(listed)
        ]

    def send_rims(grid, s, send, recv):
        for goes, _, copy in rims(grid, s, send, recv):
            pl.when(goes)(copy.start)

    def await_rims(grid, s, send, recv):
        for _, comes, copy in rims(grid, s, send, recv):
            pl.when(comes)(copy.wait_recv)

    def prepare(s):
        load(s).wait()
        for h in range(4):
            block = raw[s, 16 * h : 16 * h + 16].reshape(256, 128)
            turned = dot(block, perm).reshape(16, 16, 128)
            turned = jnp.swapaxes(turned, 0, 1).astype(BF16)
            for x in range(2):
                fg[s, 1 + x, 1:9, 16 * h : 16 * h + 16, :] = turned[8 * x : 8 * x + 8]

    def coarse_copy(s):
        return remote(
            red.at[s], coarse.at[mx, pl.ds(my * 4, 4)], r_send.at[s], r_recv.at[mine], (bx + s // 2, by + s % 2)
        )

    def coarse_arrival(s):
        return remote(
            red.at[s], coarse.at[s // 2, pl.ds(s % 2 * 4, 4)], r_send.at[s], r_recv.at[s], (ix, iy)
        )

    def own_coarse():
        return pltpu.make_async_copy(red.at[mine], coarse.at[mx, pl.ds(my * 4, 4)], own_sem)

    for s in range(2):
        prepare(s)
    pl.semaphore_wait(barrier, len(peers))
    pl.when(mine < 2)(send_cot)
    for s in range(2):
        send_rims(fg, s, f_send, f_recv)

    @pl.loop(0, S)
    def _(s):
        @pl.when(s < S - 2)
        def _():
            prepare(s + 2)
            pl.when(mine == s + 2)(send_cot)
            send_rims(fg, s + 2, f_send, f_recv)

        await_rims(fg, s, f_send, f_recv)

        @pl.when(s != mine)
        def _():
            cot_arrival(s).wait_recv()

        @pl.loop(0, 4)
        def _(j):
            down = gdn[s, j]
            none = jnp.zeros_like(down)
            down = jnp.concatenate(
                [jnp.concatenate([down, none], axis=1), jnp.concatenate([none, down], axis=1)], axis=0
            )
            gm_all = dot(w2t[...], down, NT).astype(BF16)
            depth = conv(fg, mats, s, j)
            stacked, lefts = [], []
            for x in range(2):
                dep = depth[x].astype(BF16)
                gm_x = jnp.concatenate(
                    [gm_all[128 * x : 128 * x + 64], gm_all[128 * x + 64 : 128 * x + 128]], axis=1
                )
                pre_x, grad_x = dot(pin[...], dep), dot(pout_t[...], gm_x)
                acts, gpres = [], []
                for h in range(0, HID, 64):
                    pre, grad = pre_x[h : h + 64], grad_x[h : h + 64]
                    sq = pre * pre
                    t = jnp.tanh(pre * (G0 + G1 * sq))
                    up = 0.5 + 0.5 * t
                    acts.append((pre * up).astype(BF16))
                    slope = up + 0.5 * pre * (1.0 - t * t) * (G0 + 3 * G1 * sq)
                    gpres.append((grad * slope).astype(BF16))
                act, gpre = jnp.concatenate(acts, axis=0), jnp.concatenate(gpres, axis=0)
                own = jnp.concatenate(
                    [fg[s, 1 + x, 1 + 2 * j + yy].astype(F32) for yy in range(2)], axis=1
                )
                merged = (own + dot(pout[...], act)).astype(BF16)
                stacked += [merged[:, :128], merged[:, 128:]]
                add(0, dot(gm_x, act, NT))
                add(128, dot(dep, gpre, NT))
                gdep = dot(pin_t[...], gpre).astype(BF16)
                sides = []
                for yy in range(2):
                    part = gdep[:, 128 * yy : 128 * yy + 128]
                    dg[s, 1 + x, 1 + 2 * j + yy] = part
                    gm[s, x, 2 * j + yy] = gm_x[:, 128 * yy : 128 * yy + 128]
                    here = part.astype(F32)
                    none = jnp.zeros_like(here)
                    sides.append((shifted_sum(none, none, here), here, shifted_sum(here, none, none)))
                for e in range(3):
                    lefts.append(jnp.concatenate([sides[0][e], sides[1][e]], axis=1).astype(BF16))
            for g in range(4):
                left = jnp.concatenate([m[16 * g : 16 * g + 16] for m in lefts], axis=0)
                dwacc[g] += dot(left, taps(fg, s, j, g), NT)
            stacked = jnp.concatenate(stacked, axis=0)
            add(256, dot(stacked, down))
            both = dot(stacked, w2t[...], TN)
            red[s, j] = (both[:64, :128] + both[64:, 128:]).astype(BF16)

        send_rims(dg, s, d_send, d_recv)

        @pl.when(s != mine)
        def _():
            coarse_copy(s).start()

    own_coarse().start()

    spot = lax.broadcasted_iota(jnp.int32, (192, 128), 0)
    tap = lax.broadcasted_iota(jnp.int32, (192, 128), 1)
    found = jnp.zeros((C, 128), F32)
    for q in range(6):
        a = spot // 48 - q // 3
        picks = (tap == 9 * a + 3 * (spot // 16 % 3) + q % 3) & (a >= 0) & (a <= 2)
        block = jnp.concatenate(
            [jnp.where(diag, dwacc[g, 16 * q : 16 * q + 16, :], 0.0) for g in range(4)], axis=0
        )
        found += lax.dot_general(
            block, picks.astype(F32), NN, precision=lax.Precision.HIGHEST, preferred_element_type=F32
        )
    wacc[768:832] = found

    def block(start, rows):
        return pl.ds(pl.multiple_of(start, 8), rows)

    def other(k):
        return (chip + k) % 8

    def pair_copy():
        give = block((1 - core) * HALF, HALF)
        return remote(wacc.at[give], pair, pair_send.at[0], pair_recv.at[0], (ix + 1 - 2 * core, iy))

    def rs_copy(k):
        give = block(core * HALF + other(k) * PART, PART)
        return remote(wacc.at[give], rs.at[chip], rs_send.at[k], rs_recv.at[8 - k], (2 * other(k) + core, iy))

    def rs_arrival(k):
        give = block(core * HALF, PART)
        return remote(wacc.at[give], rs.at[other(k)], rs_send.at[k], rs_recv.at[k], (ix, iy))

    def gy_copy(k):
        return remote(gyb.at[iy], gyb.at[iy], gy_send.at[k], gy_recv.at[NGY - k], (ix, (iy + k) % NGY))

    def gy_arrival(k):
        slot = (iy + k) % NGY
        return remote(gyb.at[slot], gyb.at[slot], gy_send.at[k], gy_recv.at[k], (ix, iy))

    def ag_copy(k):
        rows = block(core * HALF + chip * PART, PART)
        return remote(tot.at[rows], tot.at[rows], ag_send.at[k], ag_recv.at[8 - k], (2 * other(k) + core, iy))

    def ag_arrival(k):
        rows = block(core * HALF + other(k) * PART, PART)
        return remote(tot.at[rows], tot.at[rows], ag_send.at[k], ag_recv.at[k], (ix, iy))

    def last_copy():
        rows = block(core * HALF, HALF)
        return remote(tot.at[rows], tot.at[rows], pair_send.at[1], pair_recv.at[1], (ix + 1 - 2 * core, iy))

    def last_arrival():
        rows = block((1 - core) * HALF, HALF)
        return remote(tot.at[rows], tot.at[rows], pair_send.at[1], pair_recv.at[1], (ix, iy))

    def total(buffer):
        result = buffer[0]
        for q in range(1, 8):
            result = result + buffer[q]
        return result

    pair_copy().start()

    @pl.loop(0, S)
    def _(s):
        await_rims(dg, s, d_send, d_recv)

        @pl.loop(0, 4)
        def _(j):
            adjoint = conv(dg, mats_t, s, j)
            for x in range(2):
                for yy in range(2):
                    at = 2 * j + yy
                    summed = gm[s, x, at].astype(F32) + adjoint[x][:, 128 * yy : 128 * yy + 128]
                    back = dot(summed.astype(BF16), perm, NT)
                    swap[8 * x + at] = back

        for h in range(4):
            turned = jnp.swapaxes(swap[:, 16 * h : 16 * h + 16, :], 0, 1)
            grad_out[s, 16 * h : 16 * h + 16] = turned.astype(BF16)

        @pl.when(s == 0)
        def _():
            pair_copy().wait_recv()
            wacc[block(core * HALF, HALF)] += pair[...]
            for k in range(1, 8):
                rs_copy(k).start()

        @pl.when(s == 2)
        def _():
            rs[chip] = wacc[block(core * HALF + chip * PART, PART)]
            for k in range(1, 8):
                rs_arrival(k).wait_recv()
            gyb[iy] = total(rs)
            for k in range(1, NGY):
                gy_copy(k).start()

        @pl.when(s == 4)
        def _():
            for k in range(1, NGY):
                gy_arrival(k).wait_recv()
            tot[block(core * HALF + chip * PART, PART)] = total(gyb) * SCALE
            for k in range(1, 8):
                ag_copy(k).start()

        @pl.when(s == 6)
        def _():
            for k in range(1, 8):
                ag_arrival(k).wait_recv()
            last_copy().start()

    last_arrival().wait_recv()
    for out, at in ((grad_po, 0), (grad_in, 128)):
        out[:, :128] = tot[at : at + 64]
        out[:, 128:] = tot[at + 64 : at + 128]
    for k in range(8):
        at = 256 + 256 * (k % 2) + 64 * (k // 2)
        grad_down[pl.ds(k, 64, stride=8), :] = tot[at : at + 64]
    dw_out[...] = tot[768:832].T[:27]

    own_coarse().wait()

    @pl.loop(0, S)
    def _(s):
        @pl.when(s != mine)
        def _():
            coarse_arrival(s).wait_recv()
            coarse_copy(s).wait_send()

        for grid, send, recv in ((fg, f_send, f_recv), (dg, d_send, d_recv)):
            for goes, _, copy in rims(grid, s, send, recv):
                pl.when(goes)(copy.wait_send)

    for k in range(1, 8):
        cot_copy(k).wait_send()
        rs_copy(k).wait_send()
        ag_copy(k).wait_send()
        gy_copy(k).wait_send()
    pair_copy().wait_send()
    last_copy().wait_send()


def per_device(fields, depth_kernel, point_in, point_out, down_kernel, cotangent):
    raw = fields.reshape(S, C, 16, 128)
    cot = cotangent[0, 0, 0].transpose(1, 2, 3, 0)
    taps_in = depth_kernel.transpose(1, 2, 3, 0).reshape(27, C)
    down_in = down_kernel.transpose(1, 2, 3, 4, 0).reshape(8 * C, C2)
    vmem = pl.BlockSpec(memory_space=pltpu.VMEM)
    dma = pltpu.SemaphoreType.DMA
    hbm = pl.BlockSpec(memory_space=pl.ANY)
    coarse, grad, grad_in, grad_po, grad_down, dw = pl.pallas_call(
        kernel,
        out_shape=(
            jax.ShapeDtypeStruct((4, 8, 64, 128), BF16),
            jax.ShapeDtypeStruct((S, C, 16, 128), BF16),
            jax.ShapeDtypeStruct((C, HID), F32),
            jax.ShapeDtypeStruct((C, HID), F32),
            jax.ShapeDtypeStruct((8 * C, C2), F32),
            jax.ShapeDtypeStruct((27, C), F32),
        ),
        in_specs=[hbm] + [vmem] * 5,
        out_specs=[vmem] * 6,
        scratch_shapes=[
            pltpu.VMEM((S, C, 16, 128), BF16),
            pltpu.VMEM((HID, C), BF16),
            pltpu.VMEM((HID, C), BF16),
            pltpu.VMEM((256, 256), BF16),
            pltpu.VMEM((8 * C, C2), F32),
            pltpu.VMEM((S, 4, 10, C, 128), BF16),
            pltpu.VMEM((S, 4, 10, C, 128), BF16),
            pltpu.VMEM((S, 2, 8, C, 128), BF16),
            pltpu.VMEM((S, 4, 64, 128), BF16),
            pltpu.VMEM((S, 4, 64, 128), BF16),
            pltpu.VMEM((4, 96, 192), BF16),
            pltpu.VMEM((4, 96, 192), BF16),
            pltpu.VMEM((2 * HALF, 128), F32),
            pltpu.VMEM((4, 96, 192), F32),
            pltpu.VMEM((16, C, 128), F32),
            pltpu.VMEM((HALF, 128), F32),
            pltpu.VMEM((8, PART, 128), F32),
            pltpu.VMEM((NGY, PART, 128), F32),
            pltpu.VMEM((2 * HALF, 128), F32),
            dma((S, 8)), dma((S, 8)), dma((S, 8)), dma((S, 8)),
            dma((8,)), dma((8,)), dma((8,)), dma((8,)),
            dma((8,)), dma((8,)), dma((NGY,)), dma((NGY,)), dma((8,)), dma((8,)), dma((2,)), dma((2,)),
            dma, dma((S,)),
        ],
        compiler_params=pltpu.CompilerParams(
            collective_id=0, has_side_effects=True, vmem_limit_bytes=56 * 2**20
        ),
    )(raw, cot, taps_in, point_in.T, point_out, down_in)
    coarse = coarse.transpose(3, 0, 1, 2)[None, None, None]
    grad_down = grad_down.reshape(C, 2, 2, 2, C2).transpose(4, 0, 1, 2, 3)
    dw = dw.reshape(3, 3, 3, C).transpose(3, 0, 1, 2)
    return coarse, grad.reshape(fields.shape), dw, grad_in.T, grad_po, grad_down


def solution(mesh):
    split = P("gx", "gy", None, None, None, None, None)
    fine = P(None, None, "gx", "gy", None)
    return jax.shard_map(
        per_device,
        mesh=mesh,
        in_specs=(fine, P(), P(), P(), P(), split),
        out_specs=(split, fine, P(), P(), P(), P()),
        check_vma=False,
    )
```

time: 123 us -> 104 us (0.85)
  Pallas kernels: 106 us -> 93.4 us
  local copies, waits for them, and re-layouts: 14.4 us -> 9.81 us
    pallas_call x1, Pallas kernels: 106 us -> 93.4 us  [per_device(): pl.pallas_call(kernel, out_shape=(jax.ShapeDtypeStruct((4, 8, 64, 128), B...]
    slice x2 -> x0, local copies, waits for them, and re-layouts: 2.64 us -> none  [the longest x1 1.68 us: per_device(): sums[:64]]
    unnamed x9 -> x11, local copies, waits for them, and re-layouts: 7.65 us -> 7.16 us
    reshape x4 -> x2, local copies, waits for them, and re-layouts: 2.64 us -> 2.65 us  [the longest x1 1.33 us: per_device(): dw = dw.reshape(3, 3, 3, C).transpose(3, 0, 1, 2)]
where the time goes in v2:
time: 104 us
  Pallas kernels  93.4 us (90%)
  local copies, waits for them, and re-layouts  9.81 us (9%)
    pallas_call x1, Pallas kernels, per_device(): pl.pallas_call(kernel, out_shape=(jax.ShapeDtypeStruct((4, 8, 64, 128), B...  93.4 us
    unnamed x11, local copies, waits for them, and re-layouts  7.16 us

profile of v2, /device:TPU:1, one launch (start us, length us, event | category | flops | bytes accessed | tf_op | source)
XLA Modules:
  0.0 103.8 jit_solution(5196858910893704190)
XLA Ops:
  0.6 1.3 %reshape.31.taps_in = bf16[27,64]{1,0:T(8,128)(2,1)} reshape(bf16[3,3,3,64]{3,2,1,0:T(4,128)(2,1)} %bitcast.27) | data formatting | bytes 6912 | tf_op jit(solution)/shard_map/reshape | solution.py:436
  1.9 93.4 %shard_map.109 = (bf16[4,8,64,128]{3,2,1,0:T(8,128)(2,1)}, bf16[8,64,16,128]{3,2,1,0:T(8,128)(2,1)}, f32[64,256]{1,0:T(8,128)}, f32[64,256]{1,0:T(8,128)}, f32[512,128]{1,0:T(8,128)}, /*index=5*/f32[27,64]{1,0:T(8,128)}) custom-call(bf16[8,64,16,128]{3,2,1,0:T(8,128)(2,1)} %bitcast.18, bf16[4,8,64,128]{3,2,1,0:T(8,128)(2,1)} %bitcast.21, ...), custom_call_target="tpu_custom_call" | custom-call | tf_op jit(solution)/shard_map/pallas_call | solution.py:441
  95.3 1.3 %reshape.34 = f32[3,3,3,64]{3,2,1,0:T(4,128)} reshape(f32[27,64]{1,0:T(8,128)} %get-tuple-element.14) | data formatting | bytes 13824 | tf_op jit(solution)/shard_map/reshape | solution.py:484
  96.6 1.9 %copy.17 = bf16[1,1,1,128,4,8,64]{3,6,5,4,2,1,0:T(8,128)(2,1)} copy(bf16[1,1,1,128,4,8,64]{3,6,5,4,2,1,0:T(8,128)(2,1)} %bitcast.20) | data formatting | bytes 1048576
  98.5 0.0 copy-start.2
  98.5 0.0 copy-start.1
  98.5 0.0 copy-start
  98.5 3.3 %copy.18 = bf16[8,64,2,8,128]{4,3,2,1,0:T(8,128)(2,1)} copy(bf16[8,64,2,8,128]{4,3,2,1,0:T(8,128)(2,1)} %bitcast.19) | data formatting | bytes 4194304
  101.8 0.0 copy-done.2
  101.8 0.6 copy.19
  102.5 0.0 copy-done.1
  102.5 0.6 copy.20
  103.1 0.0 copy-done
  103.1 0.7 copy.21
Async XLA Ops:
  98.5 3.3 %copy-start.2 = (f32[64,256]{1,0:T(8,128)S(1)}, f32[64,256]{1,0:T(8,128)}, u32[]{:S(2)}) copy-start(f32[64,256]{1,0:T(8,128)} %get-tuple-element.15) | copy-start | bytes 196612
  98.5 4.0 %copy-start.1 = (f32[64,256]{1,0:T(8,128)S(1)}, f32[64,256]{1,0:T(8,128)}, u32[]{:S(2)}) copy-start(f32[64,256]{1,0:T(8,128)} %get-tuple-element.28) | copy-start | bytes 196612
  98.5 4.6 %copy-start = (f32[512,128]{1,0:T(8,128)S(1)}, f32[512,128]{1,0:T(8,128)}, u32[]{:S(2)}) copy-start(f32[512,128]{1,0:T(8,128)} %get-tuple-element.17) | copy-start | bytes 786436

commit v3 on v2

--- a/solution.py
+++ b/solution.py
@@ -59,23 +59,17 @@
 
 
 def kernel(
-    raw_hbm, cot, taps_in, pin_t, pout, down_in,
+    raw, cot, taps_in, pin_t, pout, down_in,
     coarse, grad_out, grad_in, grad_po, grad_down, dw_out,
-    raw, pin, pout_t, w2t, wide,
-    fg, dg, gm, gdn, red, mats, mats_t, wacc, dwacc, swap, pair, rs, gyb, tot,
+    pin, pout_t, w2t, wide,
+    fg, dg, gm, gdn, red, mats, mats_t, wacc, dwacc, points, swap, pair, rs, gyb, tot,
     f_send, f_recv, d_send, d_recv, c_send, c_recv, r_send, r_recv,
-    rs_send, rs_recv, gy_send, gy_recv, ag_send, ag_recv, pair_send, pair_recv, own_sem, in_sem,
+    rs_send, rs_recv, gy_send, gy_recv, ag_send, ag_recv, pair_send, pair_recv, own_sem,
 ):
     ix, iy = lax.axis_index("gx"), lax.axis_index("gy")
     mx, my = ix % 4, iy % 2
     mine = mx * 2 + my
     bx, by = ix - mx, iy - my
-
-    def load(s):
-        return pltpu.make_async_copy(raw_hbm.at[s], raw.at[s], in_sem.at[s])
-
-    for s in range(S):
-        load(s).start()
 
     for grid in (fg, dg):
         for cond, at in ((ix == 0, 0), (ix == NGX - 1, 3)):
@@ -137,7 +131,8 @@
     diag = row == col % 16
     tap = lax.broadcasted_iota(jnp.int32, (27, 192), 0)
     spot = lax.broadcasted_iota(jnp.int32, (27, 192), 1)
-    coefficients = taps_in[...]
+    flat = taps_in[...].astype(F32)
+    coefficients = jnp.concatenate([flat[a, b] for a in range(3) for b in range(3)], axis=0).astype(BF16)
     for q in range(6):
         x, e = q // 3, q % 3
         a = spot // 48 - x
@@ -149,15 +144,11 @@
                 to[g, 16 * q : 16 * q + 16] = jnp.where(diag, spread[16 * g : 16 * g + 16], 0.0).astype(BF16)
     wacc[...] = jnp.zeros_like(wacc)
     dwacc[...] = jnp.zeros_like(dwacc)
+    points[...] = jnp.zeros_like(points)
 
     zi = lax.broadcasted_iota(jnp.int32, (128, 128), 0)
     li = lax.broadcasted_iota(jnp.int32, (128, 128), 1)
     perm = (zi == jnp.where(li < 64, 2 * li, 2 * li - 127)).astype(BF16)
-
-    def add(at, term):
-        n = term.shape[0]
-        wacc[at : at + n] += term[:, :128]
-        wacc[at + n : at + 2 * n] += term[:, 128:]
 
     def rims(grid, s, send, recv):
         whole, inner = pl.ds(1, 8), pl.ds(1, 2)
@@ -186,7 +177,6 @@
             pl.when(comes)(copy.wait_recv)
 
     def prepare(s):
-        load(s).wait()
         for h in range(4):
             block = raw[s, 16 * h : 16 * h + 16].reshape(256, 128)
             turned = dot(block, perm).reshape(16, 16, 128)
@@ -228,7 +218,7 @@
         def _():
             cot_arrival(s).wait_recv()
 
-        @pl.loop(0, 4)
+        @pl.loop(0, 4, unroll=2)
         def _(j):
             down = gdn[s, j]
             none = jnp.zeros_like(down)
@@ -259,8 +249,8 @@
                 )
                 merged = (own + dot(pout[...], act)).astype(BF16)
                 stacked += [merged[:, :128], merged[:, 128:]]
-                add(0, dot(gm_x, act, NT))
-                add(128, dot(dep, gpre, NT))
+                points[0] += dot(act, gm_x, NT)
+                points[1] += dot(gpre, dep, NT)
                 gdep = dot(pin_t[...], gpre).astype(BF16)
                 sides = []
                 for yy in range(2):
@@ -276,7 +266,9 @@
                 left = jnp.concatenate([m[16 * g : 16 * g + 16] for m in lefts], axis=0)
                 dwacc[g] += dot(left, taps(fg, s, j, g), NT)
             stacked = jnp.concatenate(stacked, axis=0)
-            add(256, dot(stacked, down))
+            term = dot(stacked, down)
+            wacc[256:512] += term[:, :128]
+            wacc[512:768] += term[:, 128:]
             both = dot(stacked, w2t[...], TN)
             red[s, j] = (both[:64, :128] + both[64:, 128:]).astype(BF16)
 
@@ -301,6 +293,7 @@
             block, picks.astype(F32), NN, precision=lax.Precision.HIGHEST, preferred_element_type=F32
         )
     wacc[768:832] = found
+    wacc[0:256] = jnp.concatenate([points[0], points[1]], axis=1)
 
     def block(start, rows):
         return pl.ds(pl.multiple_of(start, 8), rows)
@@ -355,7 +348,7 @@
     def _(s):
         await_rims(dg, s, d_send, d_recv)
 
-        @pl.loop(0, 4)
+        @pl.loop(0, 4, unroll=2)
         def _(j):
             adjoint = conv(dg, mats_t, s, j)
             for x in range(2):
@@ -400,13 +393,15 @@
             last_copy().start()
 
     last_arrival().wait_recv()
-    for out, at in ((grad_po, 0), (grad_in, 128)):
-        out[:, :128] = tot[at : at + 64]
-        out[:, 128:] = tot[at + 64 : at + 128]
+    both = tot[0:256].T
+    grad_po[...] = both[:64]
+    grad_in[...] = both[64:]
     for k in range(8):
         at = 256 + 256 * (k % 2) + 64 * (k // 2)
         grad_down[pl.ds(k, 64, stride=8), :] = tot[at : at + 64]
-    dw_out[...] = tot[768:832].T[:27]
+    flat = tot[768:832].T
+    for k in range(9):
+        dw_out[k // 3, k % 3] = flat[3 * k : 3 * k + 3]
 
     own_coarse().wait()
 
@@ -430,15 +425,26 @@
     last_copy().wait_send()
 
 
+def hand_over(*refs):
+    sems = refs[12]
+    pairs = [(i, o) for n, (i, o) in enumerate(zip(refs[:6], refs[6:12])) if n != 1]
+    pairs += [(refs[1].at[s], refs[7].at[s]) for s in range(S)]
+    copies = [pltpu.make_async_copy(i, o, sems.at[n]) for n, (i, o) in enumerate(pairs)]
+    for copy in copies:
+        copy.start()
+    for copy in copies:
+        copy.wait()
+
+
 def per_device(fields, depth_kernel, point_in, point_out, down_kernel, cotangent):
     raw = fields.reshape(S, C, 16, 128)
     cot = cotangent[0, 0, 0].transpose(1, 2, 3, 0)
-    taps_in = depth_kernel.transpose(1, 2, 3, 0).reshape(27, C)
+    taps_in = depth_kernel.transpose(1, 2, 3, 0)
     down_in = down_kernel.transpose(1, 2, 3, 4, 0).reshape(8 * C, C2)
     vmem = pl.BlockSpec(memory_space=pltpu.VMEM)
     dma = pltpu.SemaphoreType.DMA
     hbm = pl.BlockSpec(memory_space=pl.ANY)
-    coarse, grad, grad_in, grad_po, grad_down, dw = pl.pallas_call(
+    results = pl.pallas_call(
         kernel,
         out_shape=(
             jax.ShapeDtypeStruct((4, 8, 64, 128), BF16),
@@ -446,12 +452,11 @@
             jax.ShapeDtypeStruct((C, HID), F32),
             jax.ShapeDtypeStruct((C, HID), F32),
             jax.ShapeDtypeStruct((8 * C, C2), F32),
-            jax.ShapeDtypeStruct((27, C), F32),
+            jax.ShapeDtypeStruct((3, 3, 3, C), F32),
         ),
-        in_specs=[hbm] + [vmem] * 5,
+        in_specs=[vmem] * 6,
         out_specs=[vmem] * 6,
         scratch_shapes=[
-            pltpu.VMEM((S, C, 16, 128), BF16),
             pltpu.VMEM((HID, C), BF16),
             pltpu.VMEM((HID, C), BF16),
             pltpu.VMEM((256, 256), BF16),
@@ -465,6 +470,7 @@
             pltpu.VMEM((4, 96, 192), BF16),
             pltpu.VMEM((2 * HALF, 128), F32),
             pltpu.VMEM((4, 96, 192), F32),
+            pltpu.VMEM((2, 256, 64), F32),
             pltpu.VMEM((16, C, 128), F32),
             pltpu.VMEM((HALF, 128), F32),
             pltpu.VMEM((8, PART, 128), F32),
@@ -473,15 +479,24 @@
             dma((S, 8)), dma((S, 8)), dma((S, 8)), dma((S, 8)),
             dma((8,)), dma((8,)), dma((8,)), dma((8,)),
             dma((8,)), dma((8,)), dma((NGY,)), dma((NGY,)), dma((8,)), dma((8,)), dma((2,)), dma((2,)),
-            dma, dma((S,)),
+            dma,
         ],
         compiler_params=pltpu.CompilerParams(
-            collective_id=0, has_side_effects=True, vmem_limit_bytes=56 * 2**20
+            collective_id=0, has_side_effects=True, vmem_limit_bytes=36 * 2**20
         ),
     )(raw, cot, taps_in, point_in.T, point_out, down_in)
+    coarse, grad, grad_in, grad_po, grad_down, dw = pl.pallas_call(
+        hand_over,
+        out_shape=[jax.ShapeDtypeStruct(r.shape, r.dtype) for r in results],
+        in_specs=[hbm] * 6,
+        out_specs=[hbm] * 6,
+        scratch_shapes=[dma((S + 5,))],
+        compiler_params=pltpu.CompilerParams(vmem_limit_bytes=2**20),
+        cost_estimate=pl.CostEstimate(flops=0, bytes_accessed=2**23, transcendentals=0),
+    )(*results)
     coarse = coarse.transpose(3, 0, 1, 2)[None, None, None]
     grad_down = grad_down.reshape(C, 2, 2, 2, C2).transpose(4, 0, 1, 2, 3)
-    dw = dw.reshape(3, 3, 3, C).transpose(3, 0, 1, 2)
+    dw = dw.transpose(3, 0, 1, 2)
     return coarse, grad.reshape(fields.shape), dw, grad_in.T, grad_po, grad_down
 
 

time: 104 us -> 94.6 us (0.910)
  Pallas kernels: 93.4 us -> 87.8 us
  local copies, waits for them, and re-layouts: 9.81 us -> 5.74 us
    pallas_call x1, Pallas kernels: 93.4 us -> 86 us  [per_device(): pl.pallas_call(kernel, out_shape=(jax.ShapeDtypeStruct((4, 8, 64, 128), B...]
    reshape x2 -> x0, local copies, waits for them, and re-layouts: 2.65 us -> none  [the longest x1 1.33 us: per_device(): dw = dw.reshape(3, 3, 3, C).transpose(3, 0, 1, 2)]
    pallas_call x0 -> x1, Pallas kernels: none -> 1.73 us  [per_device(): pl.pallas_call(hand_over, out_shape=[jax.ShapeDtypeStruct(r.shape, r.dtyp...]
    unnamed x11 -> x12, local copies, waits for them, and re-layouts: 7.16 us -> 5.74 us
where the time goes in v3:
time: 94.6 us; the launch traced here: 94.2 us
  Pallas kernels  87.8 us (93%)
  local copies, waits for them, and re-layouts  5.74 us (6%)
    pallas_call x1, Pallas kernels, per_device(): pl.pallas_call(kernel, out_shape=(jax.ShapeDtypeStruct((4, 8, 64, 128), B...  86 us
    unnamed x12, local copies, waits for them, and re-layouts  5.74 us

profile of v3, /device:TPU:1, one launch (start us, length us, event | category | flops | bytes accessed | tf_op | source)
XLA Modules:
  0.0 94.2 jit_solution(16087493522960711005)
XLA Ops:
  0.6 0.0 copy-start
  0.6 1.6 %copy-done = bf16[8,64,2,8,128]{4,3,2,1,0:T(8,128)(2,1)S(1)} copy-done((bf16[8,64,2,8,128]{4,3,2,1,0:T(8,128)(2,1)S(1)}, bf16[8,64,2,8,128]{4,3,2,1,0:T(8,128)(2,1)}, u32[]{:S(2)}) %copy-start) | copy-done | bytes 2097176
  2.2 0.0 copy-start.1
  2.2 1.0 %copy-done.1 = bf16[1,1,1,128,4,8,64]{3,6,5,4,2,1,0:T(8,128)(2,1)S(1)} copy-done((bf16[1,1,1,128,4,8,64]{3,6,5,4,2,1,0:T(8,128)(2,1)S(1)}, bf16[1,1,1,128,4,8,64]{3,6,5,4,2,1,0:T(8,128)(2,1)}, u32[]{:S(2)}) %copy-start.1) | copy-done | bytes 524312
  3.3 0.0 copy-start.2
  3.3 0.9 copy-done.2
  4.2 0.0 copy-start.3
  4.2 0.8 copy-done.3
  4.9 0.0 copy-start.4
  4.9 0.8 copy-done.4
  5.7 0.0 copy-start.5
  5.7 0.7 copy-done.5
  6.4 86.0 %shard_map.109 = (bf16[4,8,64,128]{3,2,1,0:T(8,128)(2,1)S(1)}, bf16[8,64,16,128]{3,2,1,0:T(8,128)(2,1)S(1)}, f32[64,256]{1,0:T(8,128)S(1)}, f32[64,256]{1,0:T(8,...) custom-call(bf16[8,64,16,128]{3,2,1,0:T(8,128)(2,1)S(1)} %bitcast.18, ...), custom_call_target="tpu_custom_call" | custom-call | tf_op jit(solution)/shard_map/pallas_call | solution.py:447
  92.4 1.7 %shard_map.110 = (bf16[4,8,64,128]{3,2,1,0:T(8,128)(2,1)}, bf16[8,64,16,128]{3,2,1,0:T(8,128)(2,1)}, f32[64,256]{1,0:T(8,128)}, f32[64,256]{1,0:T(8,128)}, f32[512,128]{1,0:T(8,128)}, /*index=5*/f32[3,3,3,64]{3,2,1,0:T(4,128)}) custom-call(bf16[4,8,64,128]{3,2,1,0:T(8,128)(2,1)S(1)} %get-tuple-element.18.refs_0_, ...), custom_call_target="tpu_custom_call" | custom-call | bytes 8388608 | tf_op jit(solution)/shard_map/pallas_call | solution.py:488
Async XLA Ops:
  0.6 1.6 %copy-start = (bf16[8,64,2,8,128]{4,3,2,1,0:T(8,128)(2,1)S(1)}, bf16[8,64,2,8,128]{4,3,2,1,0:T(8,128)(2,1)}, u32[]{:S(2)}) copy-start(bf16[8,64,2,8,128]{4,3,2,1,0:T(8,128)(2,1)} %param.6) | copy-start | bytes 6291460
  2.2 1.0 %copy-start.1 = (bf16[1,1,1,128,4,8,64]{3,6,5,4,2,1,0:T(8,128)(2,1)S(1)}, bf16[1,1,1,128,4,8,64]{3,6,5,4,2,1,0:T(8,128)(2,1)}, u32[]{:S(2)}) copy-start(bf16[1,1,1,128,4,8,64]{3,6,5,4,2,1,0:T(8,128)(2,1)} %param.11) | copy-start | bytes 1572868
  3.3 0.9 copy-start.2
  4.2 0.8 copy-start.3
  4.9 0.8 copy-start.4
  5.7 0.7 copy-start.5

commit v4 on v3

--- a/solution.py
+++ b/solution.py
@@ -59,34 +59,17 @@
 
 
 def kernel(
-    raw, cot, taps_in, pin_t, pout, down_in,
-    coarse, grad_out, grad_in, grad_po, grad_down, dw_out,
-    pin, pout_t, w2t, wide,
-    fg, dg, gm, gdn, red, mats, mats_t, wacc, dwacc, points, swap, pair, rs, gyb, tot,
+    raw_hbm, cot, taps_in, pin_t, pout, down_in,
+    coarse, grad_hbm, grad_in, grad_po, grad_down, dw_out,
+    raw, grad_out, pin, pout_t, w2t, wide,
+    fg, dg, gm, mg, gdn, red, mats, mats_t, wacc, dwacc, points, swap, pair, rs, gyb, tot, flat,
     f_send, f_recv, d_send, d_recv, c_send, c_recv, r_send, r_recv,
-    rs_send, rs_recv, gy_send, gy_recv, ag_send, ag_recv, pair_send, pair_recv, own_sem,
+    rs_send, rs_recv, gy_send, gy_recv, ag_send, ag_recv, pair_send, pair_recv, own_sem, in_sem, out_sem,
 ):
     ix, iy = lax.axis_index("gx"), lax.axis_index("gy")
     mx, my = ix % 4, iy % 2
     mine = mx * 2 + my
     bx, by = ix - mx, iy - my
-
-    for grid in (fg, dg):
-        for cond, at in ((ix == 0, 0), (ix == NGX - 1, 3)):
-
-            @pl.when(cond)
-            def _(grid=grid, at=at):
-                @pl.loop(0, S)
-                def _(s):
-                    grid[s, at] = jnp.zeros((10, C, 128), BF16)
-
-        for cond, at in ((iy == 0, 0), (iy == NGY - 1, 9)):
-
-            @pl.when(cond)
-            def _(grid=grid, at=at):
-                @pl.loop(0, S)
-                def _(s):
-                    grid[s, :, at] = jnp.zeros((4, C, 128), BF16)
 
     barrier = pltpu.get_barrier_semaphore()
     core, chip = ix % 2, ix // 2
@@ -98,6 +81,32 @@
     for peer in peers:
         pl.semaphore_signal(barrier, inc=1, device_id=peer, device_id_type=MESH)
 
+    def load(s):
+        return pltpu.make_async_copy(raw_hbm.at[s], raw.at[s], in_sem.at[s])
+
+    def store(s):
+        return pltpu.make_async_copy(grad_out.at[s], grad_hbm.at[s], out_sem.at[s])
+
+    for s in range(S):
+        load(s).start()
+
+    for grid in (fg, dg):
+        for cond, at in ((ix == 0, 0), (ix == NGX - 1, 3)):
+
+            @pl.when(cond)
+            def _(grid=grid, at=at):
+                @pl.loop(0, S)
+                def _(s):
+                    grid[s, at] = jnp.zeros((10, C, 128), BF16)
+
+        for cond, at in ((iy == 0, 0), (iy == NGY - 1, 9)):
+
+            @pl.when(cond)
+            def _(grid=grid, at=at):
+                @pl.loop(0, S)
+                def _(s):
+                    grid[s, :, at] = jnp.zeros((4, C, 128), BF16)
+
     def remote(src, dst, send, recv, to):
         return pltpu.make_async_remote_copy(
             src_ref=src, dst_ref=dst, send_sem=send, recv_sem=recv, device_id=to, device_id_type=MESH
@@ -117,38 +126,15 @@
         for k in range(1, 8):
             cot_copy(k).start()
 
-    gdn[mine] = cot[mx, pl.ds(my * 4, 4)]
-
-    pin[...] = pin_t[...].astype(F32).T.astype(BF16)
-    pout_t[...] = pout[...].astype(F32).T.astype(BF16)
-    wide[...] = down_in[...].astype(F32)
-    for k in range(8):
-        at = 64 * (k // 2)
-        w2t[at : at + 64, k % 2 * 128 : k % 2 * 128 + 128] = wide[pl.ds(k, 64, stride=8), :].astype(BF16)
-
-    row = lax.broadcasted_iota(jnp.int32, (16, 192), 0)
-    col = lax.broadcasted_iota(jnp.int32, (16, 192), 1)
-    diag = row == col % 16
-    tap = lax.broadcasted_iota(jnp.int32, (27, 192), 0)
-    spot = lax.broadcasted_iota(jnp.int32, (27, 192), 1)
-    flat = taps_in[...].astype(F32)
-    coefficients = jnp.concatenate([flat[a, b] for a in range(3) for b in range(3)], axis=0).astype(BF16)
-    for q in range(6):
-        x, e = q // 3, q % 3
-        a = spot // 48 - x
-        at = 9 * a + 3 * (spot // 16 % 3) + e
-        inside = (a >= 0) & (a <= 2)
-        for to, place in ((mats, at), (mats_t, 26 - at)):
-            spread = dot(coefficients, ((tap == place) & inside).astype(BF16), TN)
-            for g in range(4):
-                to[g, 16 * q : 16 * q + 16] = jnp.where(diag, spread[16 * g : 16 * g + 16], 0.0).astype(BF16)
-    wacc[...] = jnp.zeros_like(wacc)
-    dwacc[...] = jnp.zeros_like(dwacc)
-    points[...] = jnp.zeros_like(points)
+    def own_cot():
+        return pltpu.make_async_copy(cot.at[mx, pl.ds(my * 4, 4)], gdn.at[mine], own_sem.at[1])
+
+    own_cot().start()
 
     zi = lax.broadcasted_iota(jnp.int32, (128, 128), 0)
     li = lax.broadcasted_iota(jnp.int32, (128, 128), 1)
     perm = (zi == jnp.where(li < 64, 2 * li, 2 * li - 127)).astype(BF16)
+    unperm = (li == jnp.where(zi < 64, 2 * zi, 2 * zi - 127)).astype(BF16)
 
     def rims(grid, s, send, recv):
         whole, inner = pl.ds(1, 8), pl.ds(1, 2)
@@ -177,6 +163,7 @@
             pl.when(comes)(copy.wait_recv)
 
     def prepare(s):
+        load(s).wait()
         for h in range(4):
             block = raw[s, 16 * h : 16 * h + 16].reshape(256, 128)
             turned = dot(block, perm).reshape(16, 16, 128)
@@ -195,7 +182,7 @@
         )
 
     def own_coarse():
-        return pltpu.make_async_copy(red.at[mine], coarse.at[mx, pl.ds(my * 4, 4)], own_sem)
+        return pltpu.make_async_copy(red.at[mine], coarse.at[mx, pl.ds(my * 4, 4)], own_sem.at[0])
 
     for s in range(2):
         prepare(s)
@@ -204,6 +191,33 @@
     for s in range(2):
         send_rims(fg, s, f_send, f_recv)
 
+    pin[...] = pin_t[...].astype(F32).T.astype(BF16)
+    pout_t[...] = pout[...].astype(F32).T.astype(BF16)
+    wide[...] = down_in[...].astype(F32)
+    for k in range(8):
+        at = 64 * (k // 2)
+        w2t[at : at + 64, k % 2 * 128 : k % 2 * 128 + 128] = wide[pl.ds(k, 64, stride=8), :].astype(BF16)
+
+    row = lax.broadcasted_iota(jnp.int32, (16, 192), 0)
+    col = lax.broadcasted_iota(jnp.int32, (16, 192), 1)
+    diag = row == col % 16
+    tap = lax.broadcasted_iota(jnp.int32, (27, 192), 0)
+    spot = lax.broadcasted_iota(jnp.int32, (27, 192), 1)
+    given = taps_in[...].astype(F32)
+    coefficients = jnp.concatenate([given[a, b] for a in range(3) for b in range(3)], axis=0).astype(BF16)
+    for q in range(6):
+        x, e = q // 3, q % 3
+        a = spot // 48 - x
+        at = 9 * a + 3 * (spot // 16 % 3) + e
+        inside = (a >= 0) & (a <= 2)
+        for to, place in ((mats, at), (mats_t, 26 - at)):
+            spread = dot(coefficients, ((tap == place) & inside).astype(BF16), TN)
+            for g in range(4):
+                to[g, 16 * q : 16 * q + 16] = jnp.where(diag, spread[16 * g : 16 * g + 16], 0.0).astype(BF16)
+    wacc[...] = jnp.zeros_like(wacc)
+    dwacc[...] = jnp.zeros_like(dwacc)
+    points[...] = jnp.zeros_like(points)
+
     @pl.loop(0, S)
     def _(s):
         @pl.when(s < S - 2)
@@ -218,67 +232,76 @@
         def _():
             cot_arrival(s).wait_recv()
 
-        @pl.loop(0, 4, unroll=2)
-        def _(j):
-            down = gdn[s, j]
-            none = jnp.zeros_like(down)
-            down = jnp.concatenate(
-                [jnp.concatenate([down, none], axis=1), jnp.concatenate([none, down], axis=1)], axis=0
-            )
-            gm_all = dot(w2t[...], down, NT).astype(BF16)
-            depth = conv(fg, mats, s, j)
-            stacked, lefts = [], []
-            for x in range(2):
-                dep = depth[x].astype(BF16)
-                gm_x = jnp.concatenate(
-                    [gm_all[128 * x : 128 * x + 64], gm_all[128 * x + 64 : 128 * x + 128]], axis=1
-                )
-                pre_x, grad_x = dot(pin[...], dep), dot(pout_t[...], gm_x)
-                acts, gpres = [], []
-                for h in range(0, HID, 64):
-                    pre, grad = pre_x[h : h + 64], grad_x[h : h + 64]
-                    sq = pre * pre
-                    t = jnp.tanh(pre * (G0 + G1 * sq))
-                    up = 0.5 + 0.5 * t
-                    acts.append((pre * up).astype(BF16))
-                    slope = up + 0.5 * pre * (1.0 - t * t) * (G0 + 3 * G1 * sq)
-                    gpres.append((grad * slope).astype(BF16))
-                act, gpre = jnp.concatenate(acts, axis=0), jnp.concatenate(gpres, axis=0)
-                own = jnp.concatenate(
-                    [fg[s, 1 + x, 1 + 2 * j + yy].astype(F32) for yy in range(2)], axis=1
-                )
-                merged = (own + dot(pout[...], act)).astype(BF16)
-                stacked += [merged[:, :128], merged[:, 128:]]
-                points[0] += dot(act, gm_x, NT)
-                points[1] += dot(gpre, dep, NT)
-                gdep = dot(pin_t[...], gpre).astype(BF16)
-                sides = []
-                for yy in range(2):
-                    part = gdep[:, 128 * yy : 128 * yy + 128]
-                    dg[s, 1 + x, 1 + 2 * j + yy] = part
-                    gm[s, x, 2 * j + yy] = gm_x[:, 128 * yy : 128 * yy + 128]
-                    here = part.astype(F32)
-                    none = jnp.zeros_like(here)
-                    sides.append((shifted_sum(none, none, here), here, shifted_sum(here, none, none)))
-                for e in range(3):
-                    lefts.append(jnp.concatenate([sides[0][e], sides[1][e]], axis=1).astype(BF16))
-            for g in range(4):
-                left = jnp.concatenate([m[16 * g : 16 * g + 16] for m in lefts], axis=0)
-                dwacc[g] += dot(left, taps(fg, s, j, g), NT)
-            stacked = jnp.concatenate(stacked, axis=0)
-            term = dot(stacked, down)
+        @pl.when(s == mine)
+        def _():
+            own_cot().wait()
+
+        @pl.loop(0, 2)
+        def _(pair_of):
+            downs = []
+            for jj in range(2):
+                down = gdn[s, 2 * pair_of + jj]
+                none = jnp.zeros_like(down)
+                downs += [jnp.concatenate([down, none], axis=1), jnp.concatenate([none, down], axis=1)]
+            downs = jnp.concatenate(downs, axis=0)
+            gm_all = dot(w2t[...], downs, NT).astype(BF16)
+            pools = ([], [], [], [])
+            stacks = []
+            lefts = [[], [], [], [], [], []]
+            for jj in range(2):
+                j = 2 * pair_of + jj
+                gm_j = gm_all[:, 128 * jj : 128 * jj + 128]
+                depth = conv(fg, mats, s, j)
+                stacked = []
+                for x in range(2):
+                    dep = depth[x].astype(BF16)
+                    gm_x = jnp.concatenate(
+                        [gm_j[128 * x : 128 * x + 64], gm_j[128 * x + 64 : 128 * x + 128]], axis=1
+                    )
+                    pre_x, grad_x = dot(pin[...], dep), dot(pout_t[...], gm_x)
+                    acts, gpres = [], []
+                    for h in range(0, HID, 64):
+                        pre, grad = pre_x[h : h + 64], grad_x[h : h + 64]
+                        sq = pre * pre
+                        t = jnp.tanh(pre * (G0 + G1 * sq))
+                        up = 0.5 + 0.5 * t
+                        acts.append((pre * up).astype(BF16))
+                        slope = up + 0.5 * pre * (1.0 - t * t) * (G0 + 3 * G1 * sq)
+                        gpres.append((grad * slope).astype(BF16))
+                    act, gpre = jnp.concatenate(acts, axis=0), jnp.concatenate(gpres, axis=0)
+                    own = jnp.concatenate(
+                        [fg[s, 1 + x, 1 + 2 * j + yy].astype(F32) for yy in range(2)], axis=1
+                    )
+                    merged = (own + dot(pout[...], act)).astype(BF16)
+                    stacked += [merged[:, :128], merged[:, 128:]]
+                    for pool, part in zip(pools, (act, gm_x, gpre, dep)):
+                        pool.append(part)
+                    gdep = dot(pin_t[...], gpre).astype(BF16)
+                    for yy in range(2):
+                        part = gdep[:, 128 * yy : 128 * yy + 128]
+                        dg[s, 1 + x, 1 + 2 * j + yy] = part
+                        gm[s, x, 2 * j + yy] = gm_x[:, 128 * yy : 128 * yy + 128]
+                        here = part.astype(F32)
+                        none = jnp.zeros_like(here)
+                        lefts[3 * x].append(shifted_sum(none, none, here).astype(BF16))
+                        lefts[3 * x + 1].append(part)
+                        lefts[3 * x + 2].append(shifted_sum(here, none, none).astype(BF16))
+                stacked = jnp.concatenate(stacked, axis=0)
+                mg[s, j] = stacked
+                stacks.append(stacked)
+            act, gm_x, gpre, dep = (jnp.concatenate(pool, axis=1) for pool in pools)
+            points[0] += dot(act, gm_x, NT)
+            points[1] += dot(gpre, dep, NT)
+            term = dot(jnp.concatenate(stacks, axis=1), downs)
             wacc[256:512] += term[:, :128]
             wacc[512:768] += term[:, 128:]
-            both = dot(stacked, w2t[...], TN)
-            red[s, j] = (both[:64, :128] + both[64:, 128:]).astype(BF16)
+            lines = [jnp.concatenate(line, axis=1) for line in lefts]
+            for g in range(4):
+                left = jnp.concatenate([m[16 * g : 16 * g + 16] for m in lines], axis=0)
+                right = [taps(fg, s, 2 * pair_of + jj, g) for jj in range(2)]
+                dwacc[g] += dot(left, jnp.concatenate(right, axis=1), NT)
 
         send_rims(dg, s, d_send, d_recv)
-
-        @pl.when(s != mine)
-        def _():
-            coarse_copy(s).start()
-
-    own_coarse().start()
 
     spot = lax.broadcasted_iota(jnp.int32, (192, 128), 0)
     tap = lax.broadcasted_iota(jnp.int32, (192, 128), 1)
@@ -321,19 +344,19 @@
         return remote(gyb.at[slot], gyb.at[slot], gy_send.at[k], gy_recv.at[k], (ix, iy))
 
     def ag_copy(k):
-        rows = block(core * HALF + chip * PART, PART)
-        return remote(tot.at[rows], tot.at[rows], ag_send.at[k], ag_recv.at[8 - k], (2 * other(k) + core, iy))
+        slot = core * 8 + chip
+        return remote(tot.at[slot], tot.at[slot], ag_send.at[k], ag_recv.at[8 - k], (2 * other(k) + core, iy))
 
     def ag_arrival(k):
-        rows = block(core * HALF + other(k) * PART, PART)
-        return remote(tot.at[rows], tot.at[rows], ag_send.at[k], ag_recv.at[k], (ix, iy))
+        slot = core * 8 + other(k)
+        return remote(tot.at[slot], tot.at[slot], ag_send.at[k], ag_recv.at[k], (ix, iy))
 
     def last_copy():
-        rows = block(core * HALF, HALF)
+        rows = pl.ds(core * 8, 8)
         return remote(tot.at[rows], tot.at[rows], pair_send.at[1], pair_recv.at[1], (ix + 1 - 2 * core, iy))
 
     def last_arrival():
-        rows = block((1 - core) * HALF, HALF)
+        rows = pl.ds(8 - core * 8, 8)
         return remote(tot.at[rows], tot.at[rows], pair_send.at[1], pair_recv.at[1], (ix, iy))
 
     def total(buffer):
@@ -344,6 +367,31 @@
 
     pair_copy().start()
 
+    def reduce(s):
+        rows = jnp.concatenate([mg[s, j] for j in range(4)], axis=1)
+        both = dot(rows, w2t[...], TN)
+        for j in range(4):
+            at = 128 * j
+            red[s, j] = (both[at : at + 64, :128] + both[at + 64 : at + 128, 128:]).astype(BF16)
+
+    def send_coarse(s):
+        @pl.when(s != mine)
+        def _():
+            coarse_copy(s).start()
+
+        @pl.when(s == mine)
+        def _():
+            own_coarse().start()
+
+    for s in range(2):
+        reduce(s)
+    pair_copy().wait_recv()
+    wacc[block(core * HALF, HALF)] += pair[...]
+    for k in range(1, 8):
+        rs_copy(k).start()
+    for s in range(2):
+        send_coarse(s)
+
     @pl.loop(0, S)
     def _(s):
         await_rims(dg, s, d_send, d_recv)
@@ -351,23 +399,27 @@
         @pl.loop(0, 4, unroll=2)
         def _(j):
             adjoint = conv(dg, mats_t, s, j)
+            sides = []
             for x in range(2):
                 for yy in range(2):
-                    at = 2 * j + yy
-                    summed = gm[s, x, at].astype(F32) + adjoint[x][:, 128 * yy : 128 * yy + 128]
-                    back = dot(summed.astype(BF16), perm, NT)
-                    swap[8 * x + at] = back
+                    summed = gm[s, x, 2 * j + yy].astype(F32) + adjoint[x][:, 128 * yy : 128 * yy + 128]
+                    sides.append(summed.astype(BF16))
+            back = dot(jnp.concatenate(sides, axis=0), unperm)
+            for x in range(2):
+                for yy in range(2):
+                    at = 128 * x + 64 * yy
+                    swap[8 * x + 2 * j + yy] = back[at : at + 64]
 
         for h in range(4):
             turned = jnp.swapaxes(swap[:, 16 * h : 16 * h + 16, :], 0, 1)
             grad_out[s, 16 * h : 16 * h + 16] = turned.astype(BF16)
-
-        @pl.when(s == 0)
-        def _():
-            pair_copy().wait_recv()
-            wacc[block(core * HALF, HALF)] += pair[...]
-            for k in range(1, 8):
-                rs_copy(k).start()
+        store(s).start()
+
+        @pl.when(s < 3)
+        def _():
+            for k in range(2):
+                reduce(2 + 2 * s + k)
+                send_coarse(2 + 2 * s + k)
 
         @pl.when(s == 2)
         def _():
@@ -382,7 +434,7 @@
         def _():
             for k in range(1, NGY):
                 gy_arrival(k).wait_recv()
-            tot[block(core * HALF + chip * PART, PART)] = total(gyb) * SCALE
+            tot[core * 8 + chip] = (total(gyb) * SCALE).astype(BF16)
             for k in range(1, 8):
                 ag_copy(k).start()
 
@@ -393,15 +445,17 @@
             last_copy().start()
 
     last_arrival().wait_recv()
-    both = tot[0:256].T
+    for slot in range(16):
+        flat[PART * slot : PART * slot + PART] = tot[slot].astype(F32)
+    both = flat[0:256].T
     grad_po[...] = both[:64]
     grad_in[...] = both[64:]
     for k in range(8):
         at = 256 + 256 * (k % 2) + 64 * (k // 2)
-        grad_down[pl.ds(k, 64, stride=8), :] = tot[at : at + 64]
-    flat = tot[768:832].T
+        grad_down[pl.ds(k, 64, stride=8), :] = flat[at : at + 64]
+    lines = flat[768:832].T
     for k in range(9):
-        dw_out[k // 3, k % 3] = flat[3 * k : 3 * k + 3]
+        dw_out[k // 3, k % 3] = lines[3 * k : 3 * k + 3]
 
     own_coarse().wait()
 
@@ -412,6 +466,7 @@
             coarse_arrival(s).wait_recv()
             coarse_copy(s).wait_send()
 
+        store(s).wait()
         for grid, send, recv in ((fg, f_send, f_recv), (dg, d_send, d_recv)):
             for goes, _, copy in rims(grid, s, send, recv):
                 pl.when(goes)(copy.wait_send)
@@ -426,13 +481,17 @@
 
 
 def hand_over(*refs):
-    sems = refs[12]
-    pairs = [(i, o) for n, (i, o) in enumerate(zip(refs[:6], refs[6:12])) if n != 1]
-    pairs += [(refs[1].at[s], refs[7].at[s]) for s in range(S)]
-    copies = [pltpu.make_async_copy(i, o, sems.at[n]) for n, (i, o) in enumerate(pairs)]
-    for copy in copies:
+    held, arrive, leave = refs[12:18], refs[18], refs[19]
+    trips = [(refs[1].at[s], held[1].at[s], refs[7].at[s]) for s in range(S)]
+    trips += [(refs[n], held[n], refs[6 + n]) for n in (0, 2, 3, 4, 5)]
+    into = [pltpu.make_async_copy(a, b, arrive.at[n]) for n, (a, b, _) in enumerate(trips)]
+    out = [pltpu.make_async_copy(b, c, leave.at[n]) for n, (_, b, c) in enumerate(trips)]
+    for copy in into:
         copy.start()
-    for copy in copies:
+    for first, then in zip(into, out):
+        first.wait()
+        then.start()
+    for copy in out:
         copy.wait()
 
 
@@ -454,9 +513,11 @@
             jax.ShapeDtypeStruct((8 * C, C2), F32),
             jax.ShapeDtypeStruct((3, 3, 3, C), F32),
         ),
-        in_specs=[vmem] * 6,
-        out_specs=[vmem] * 6,
+        in_specs=[hbm] * 2 + [vmem] * 4,
+        out_specs=[vmem, hbm] + [vmem] * 4,
         scratch_shapes=[
+            pltpu.VMEM((S, C, 16, 128), BF16),
+            pltpu.VMEM((S, C, 16, 128), BF16),
             pltpu.VMEM((HID, C), BF16),
             pltpu.VMEM((HID, C), BF16),
             pltpu.VMEM((256, 256), BF16),
@@ -464,6 +525,7 @@
             pltpu.VMEM((S, 4, 10, C, 128), BF16),
             pltpu.VMEM((S, 4, 10, C, 128), BF16),
             pltpu.VMEM((S, 2, 8, C, 128), BF16),
+            pltpu.VMEM((S, 4, 256, 128), BF16),
             pltpu.VMEM((S, 4, 64, 128), BF16),
             pltpu.VMEM((S, 4, 64, 128), BF16),
             pltpu.VMEM((4, 96, 192), BF16),
@@ -475,14 +537,15 @@
             pltpu.VMEM((HALF, 128), F32),
             pltpu.VMEM((8, PART, 128), F32),
             pltpu.VMEM((NGY, PART, 128), F32),
+            pltpu.VMEM((16, PART, 128), BF16),
             pltpu.VMEM((2 * HALF, 128), F32),
             dma((S, 8)), dma((S, 8)), dma((S, 8)), dma((S, 8)),
             dma((8,)), dma((8,)), dma((8,)), dma((8,)),
             dma((8,)), dma((8,)), dma((NGY,)), dma((NGY,)), dma((8,)), dma((8,)), dma((2,)), dma((2,)),
-            dma,
+            dma((2,)), dma((S,)), dma((S,)),
         ],
         compiler_params=pltpu.CompilerParams(
-            collective_id=0, has_side_effects=True, vmem_limit_bytes=36 * 2**20
+            collective_id=0, has_side_effects=True, vmem_limit_bytes=56 * 2**20
         ),
     )(raw, cot, taps_in, point_in.T, point_out, down_in)
     coarse, grad, grad_in, grad_po, grad_down, dw = pl.pallas_call(
@@ -490,8 +553,8 @@
         out_shape=[jax.ShapeDtypeStruct(r.shape, r.dtype) for r in results],
         in_specs=[hbm] * 6,
         out_specs=[hbm] * 6,
-        scratch_shapes=[dma((S + 5,))],
-        compiler_params=pltpu.CompilerParams(vmem_limit_bytes=2**20),
+        scratch_shapes=[pltpu.VMEM(r.shape, r.dtype) for r in results] + [dma((S + 5,)), dma((S + 5,))],
+        compiler_params=pltpu.CompilerParams(vmem_limit_bytes=56 * 2**20),
         cost_estimate=pl.CostEstimate(flops=0, bytes_accessed=2**23, transcendentals=0),
     )(*results)
     coarse = coarse.transpose(3, 0, 1, 2)[None, None, None]

time: 94.6 us -> 88 us (0.930)
  local copies, waits for them, and re-layouts: 5.74 us -> 0 us
    unnamed x12 -> x0, local copies, waits for them, and re-layouts: 5.74 us -> none
    pallas_call x1, Pallas kernels: 86 us -> 84.4 us  [per_device(): pl.pallas_call(kernel, out_shape=(jax.ShapeDtypeStruct((4, 8, 64, 128), B...]
    pallas_call x1, Pallas kernels: 1.73 us -> 2.83 us  [per_device(): pl.pallas_call(hand_over, out_shape=[jax.ShapeDtypeStruct(r.shape, r.dtyp...]
where the time goes in v4:
time: 88 us; the launch traced here: 87.9 us
  Pallas kernels  87.2 us (99%)
    pallas_call x1, Pallas kernels, per_device(): pl.pallas_call(kernel, out_shape=(jax.ShapeDtypeStruct((4, 8, 64, 128), B...  84.4 us
    pallas_call x1, Pallas kernels, per_device(): pl.pallas_call(hand_over, out_shape=[jax.ShapeDtypeStruct(r.shape, r.dtyp...  2.83 us

profile of v4, /device:TPU:1, one launch (start us, length us, event | category | flops | bytes accessed | tf_op | source)
XLA Modules:
  0.0 87.9 jit_solution(17420454536552380099)
XLA Ops:
  0.6 84.4 %shard_map.109 = (bf16[4,8,64,128]{3,2,1,0:T(8,128)(2,1)}, bf16[8,64,16,128]{3,2,1,0:T(8,128)(2,1)}, f32[64,256]{1,0:T(8,128)}, f32[64,256]{1,0:T(8,128)}, f32[512,128]{1,0:T(8,128)}, /*index=5*/f32[3,3,3,64]{3,2,1,0:T(4,128)}) custom-call(bf16[8,64,16,128]{3,2,1,0:T(8,128)(2,1)} %bitcast.18, bf16[4,8,64,128]{3,2,1,0:T(8,128)(2,1)} %bitcast.19, ...), custom_call_target="tpu_custom_call" | custom-call | tf_op jit(solution)/shard_map/pallas_call | solution.py:506
  85.0 2.8 %shard_map.110 = (bf16[4,8,64,128]{3,2,1,0:T(8,128)(2,1)}, bf16[8,64,16,128]{3,2,1,0:T(8,128)(2,1)}, f32[64,256]{1,0:T(8,128)}, f32[64,256]{1,0:T(8,128)}, f32[512,128]{1,0:T(8,128)}, /*index=5*/f32[3,3,3,64]{3,2,1,0:T(4,128)}) custom-call(bf16[4,8,64,128]{3,2,1,0:T(8,128)(2,1)} %get-tuple-element.18.refs_0_, ...), custom_call_target="tpu_custom_call" | custom-call | bytes 8388608 | tf_op jit(solution)/shard_map/pallas_call | solution.py:551

commit v5 on v4

--- a/solution.py
+++ b/solution.py
@@ -236,7 +236,7 @@
         def _():
             own_cot().wait()
 
-        @pl.loop(0, 2)
+        @pl.loop(0, 2, unroll=2)
         def _(pair_of):
             downs = []
             for jj in range(2):
@@ -305,16 +305,21 @@
 
     spot = lax.broadcasted_iota(jnp.int32, (192, 128), 0)
     tap = lax.broadcasted_iota(jnp.int32, (192, 128), 1)
+    picks, blocks = [], []
+    for q in range(6):
+        a = spot // 48 - q // 3
+        picks.append(((tap == 9 * a + 3 * (spot // 16 % 3) + q % 3) & (a >= 0) & (a <= 2)).astype(BF16))
+        blocks.append(
+            jnp.concatenate([jnp.where(diag, dwacc[g, 16 * q : 16 * q + 16, :], 0.0) for g in range(4)], axis=0)
+        )
     found = jnp.zeros((C, 128), F32)
     for q in range(6):
-        a = spot // 48 - q // 3
-        picks = (tap == 9 * a + 3 * (spot // 16 % 3) + q % 3) & (a >= 0) & (a <= 2)
-        block = jnp.concatenate(
-            [jnp.where(diag, dwacc[g, 16 * q : 16 * q + 16, :], 0.0) for g in range(4)], axis=0
-        )
-        found += lax.dot_general(
-            block, picks.astype(F32), NN, precision=lax.Precision.HIGHEST, preferred_element_type=F32
-        )
+        high = blocks[q].astype(BF16)
+        rest = blocks[q] - high.astype(F32)
+        middle = rest.astype(BF16)
+        low = (rest - middle.astype(F32)).astype(BF16)
+        terms = dot(jnp.concatenate([high, middle, low], axis=0), picks[q])
+        found += terms[:64] + terms[64:128] + terms[128:]
     wacc[768:832] = found
     wacc[0:256] = jnp.concatenate([points[0], points[1]], axis=1)
 

time: 88 us -> 86.4 us (0.982)
  Pallas kernels: 87.2 us -> 85.6 us
    pallas_call x1, Pallas kernels: 84.4 us -> 82.7 us  [per_device(): pl.pallas_call(kernel, out_shape=(jax.ShapeDtypeStruct((4, 8, 64, 128), B...]
where the time goes in v5:
time: 86.4 us; the launch traced here: 86.2 us
  Pallas kernels  85.6 us (99%)
    pallas_call x1, Pallas kernels, per_device(): pl.pallas_call(kernel, out_shape=(jax.ShapeDtypeStruct((4, 8, 64, 128), B...  82.7 us
    pallas_call x1, Pallas kernels, per_device(): pl.pallas_call(hand_over, out_shape=[jax.ShapeDtypeStruct(r.shape, r.dtyp...  2.83 us

profile of v5, /device:TPU:1, one launch (start us, length us, event | category | flops | bytes accessed | tf_op | source)
XLA Modules:
  0.0 86.2 jit_solution(7816708990730204242)
XLA Ops:
  0.6 82.7 %shard_map.109 = (bf16[4,8,64,128]{3,2,1,0:T(8,128)(2,1)}, bf16[8,64,16,128]{3,2,1,0:T(8,128)(2,1)}, f32[64,256]{1,0:T(8,128)}, f32[64,256]{1,0:T(8,128)}, f32[512,128]{1,0:T(8,128)}, /*index=5*/f32[3,3,3,64]{3,2,1,0:T(4,128)}) custom-call(bf16[8,64,16,128]{3,2,1,0:T(8,128)(2,1)} %bitcast.18, bf16[4,8,64,128]{3,2,1,0:T(8,128)(2,1)} %bitcast.19, ...), custom_call_target="tpu_custom_call" | custom-call | tf_op jit(solution)/shard_map/pallas_call | solution.py:511
  83.4 2.8 %shard_map.110 = (bf16[4,8,64,128]{3,2,1,0:T(8,128)(2,1)}, bf16[8,64,16,128]{3,2,1,0:T(8,128)(2,1)}, f32[64,256]{1,0:T(8,128)}, f32[64,256]{1,0:T(8,128)}, f32[512,128]{1,0:T(8,128)}, /*index=5*/f32[3,3,3,64]{3,2,1,0:T(4,128)}) custom-call(bf16[4,8,64,128]{3,2,1,0:T(8,128)(2,1)} %get-tuple-element.18.refs_0_, ...), custom_call_target="tpu_custom_call" | custom-call | bytes 8388608 | tf_op jit(solution)/shard_map/pallas_call | solution.py:556

commit v6 on v5

--- a/solution.py
+++ b/solution.py
@@ -443,7 +443,7 @@
             for k in range(1, 8):
                 ag_copy(k).start()
 
-        @pl.when(s == 6)
+        @pl.when(s == 7)
         def _():
             for k in range(1, 8):
                 ag_arrival(k).wait_recv()

time: 86.4 us -> 86.4 us (level)
  no operation moved by 1% of the time
where the time goes in v6:
time: 86.4 us; the launch traced here: 86.2 us
  Pallas kernels  85.6 us (99%)
    pallas_call x1, Pallas kernels, per_device(): pl.pallas_call(kernel, out_shape=(jax.ShapeDtypeStruct((4, 8, 64, 128), B...  82.7 us
    pallas_call x1, Pallas kernels, per_device(): pl.pallas_call(hand_over, out_shape=[jax.ShapeDtypeStruct(r.shape, r.dtyp...  2.83 us

profile of v6, /device:TPU:1, one launch (start us, length us, event | category | flops | bytes accessed | tf_op | source)
XLA Modules:
  0.0 86.2 jit_solution(1668031587207341081)
XLA Ops:
  0.6 82.7 %shard_map.109 = (bf16[4,8,64,128]{3,2,1,0:T(8,128)(2,1)}, bf16[8,64,16,128]{3,2,1,0:T(8,128)(2,1)}, f32[64,256]{1,0:T(8,128)}, f32[64,256]{1,0:T(8,128)}, f32[512,128]{1,0:T(8,128)}, /*index=5*/f32[3,3,3,64]{3,2,1,0:T(4,128)}) custom-call(bf16[8,64,16,128]{3,2,1,0:T(8,128)(2,1)} %bitcast.18, bf16[4,8,64,128]{3,2,1,0:T(8,128)(2,1)} %bitcast.19, ...), custom_call_target="tpu_custom_call" | custom-call | tf_op jit(solution)/shard_map/pallas_call | solution.py:511
  83.4 2.8 %shard_map.110 = (bf16[4,8,64,128]{3,2,1,0:T(8,128)(2,1)}, bf16[8,64,16,128]{3,2,1,0:T(8,128)(2,1)}, f32[64,256]{1,0:T(8,128)}, f32[64,256]{1,0:T(8,128)}, f32[512,128]{1,0:T(8,128)}, /*index=5*/f32[3,3,3,64]{3,2,1,0:T(4,128)}) custom-call(bf16[4,8,64,128]{3,2,1,0:T(8,128)(2,1)} %get-tuple-element.18.refs_0_, ...), custom_call_target="tpu_custom_call" | custom-call | bytes 8388608 | tf_op jit(solution)/shard_map/pallas_call | solution.py:556
